TPU v7x, 256 devices: a whole 4x4x8 slice. The times are simulated.
256 devices in a mesh: dp: 32 (over x, z), tensor: 8 (over y, core).
Axes of the slice: x: 4, y: 4, z: 8, core: 2. Of those that a mesh axis runs over, the one named last changes fastest.
Arguments:
- tokens_in: bfloat16 [4096, 8192], P('dp'), may hold values from -6 to 6
- out_grad: bfloat16 [4096, 8192], P('dp'), may hold values from -0.25 to 0.25
- up_grad: bfloat16 [4096, 28672], P('dp', 'tensor'), may hold values from -0.25 to 0.25
- hidden_act: bfloat16 [4096, 28672], P('dp', 'tensor'), may hold values from -6 to 6
- basis_up: bfloat16 [8192, 512], P('dp'), may hold values from -0.0625 to 0.0625
- basis_down: bfloat16 [8192, 512], P('dp'), may hold values from -0.0625 to 0.0625
- moment_up: float32 [512, 28672], P('dp', 'tensor'), may hold values from -4 to 4
- second_up: float32 [512, 28672], P('dp', 'tensor'), may hold values from 0.01 to 0.1
- moment_down: float32 [512, 28672], P('dp', 'tensor'), may hold values from -4 to 4
- second_down: float32 [512, 28672], P('dp', 'tensor'), may hold values from 0.01 to 0.1
Outputs:
- delta_up: bfloat16 [8192, 28672], P('dp', 'tensor')
- delta_down: bfloat16 [28672, 8192], P('tensor', 'dp')
- next_moment_up: float32 [512, 28672], P('dp', 'tensor')
- next_second_up: float32 [512, 28672], P('dp', 'tensor')
- next_moment_down: float32 [512, 28672], P('dp', 'tensor')
- next_second_down: float32 [512, 28672], P('dp', 'tensor')
All inputs are finite; a program needn't handle non-finite values.
Results may differ from a plain program's by a relative error of at most 0.019.
Values may be sent and summed in bfloat16 or wider, within the bound.
A program may use at most 128 MiB of HBM per device.

v0:
```python
import jax
import jax.numpy as jnp
from jax import lax
from jax.sharding import PartitionSpec as P

STEPS = 1000


momentum_decay = 0.9
square_decay = 0.999
adam_epsilon = 1e-08
update_scale = 2.5


def adam_update(gradient, moment, second):
    new_moment = momentum_decay * moment + (1.0 - momentum_decay) * gradient
    new_second = square_decay * second + (1.0 - square_decay) * gradient * gradient
    first_fix = 1.0 - momentum_decay**STEPS
    second_fix = 1.0 - square_decay**STEPS
    update = (
        update_scale * (new_moment / first_fix) / (jnp.sqrt(new_second / second_fix) + adam_epsilon)
    )
    return (new_moment, new_second, update.astype(jnp.bfloat16))


def local(
    tokens_in,
    out_grad,
    up_grad,
    hidden_act,
    basis_up,
    basis_down,
    moment_up,
    second_up,
    moment_down,
    second_down,
):
    pieces = (
        lax.all_gather(basis_up, "dp", axis=0, tiled=True),
        lax.all_gather(basis_down, "dp", axis=0, tiled=True),
    )
    summed_up = jnp.dot(tokens_in, pieces[0], preferred_element_type=jnp.float32)
    summed_down = jnp.dot(out_grad, pieces[1], preferred_element_type=jnp.float32)
    proj_tokens = summed_up.astype(jnp.bfloat16)
    proj_grads = summed_down.astype(jnp.bfloat16)
    hidden_cols = up_grad.shape[1]
    contract_rows = (((0,), (0,)), ((), ()))
    term_up = lax.dot_general(
        proj_tokens, up_grad, contract_rows, preferred_element_type=jnp.float32
    )
    term_down = lax.dot_general(
        proj_grads, hidden_act, contract_rows, preferred_element_type=jnp.float32
    )
    gradients = lax.psum_scatter(
        jnp.concatenate([term_up, term_down], axis=1).astype(jnp.bfloat16),
        "dp",
        scatter_dimension=0,
        tiled=True,
    ).astype(jnp.float32)
    grad_up = gradients[:, :hidden_cols]
    grad_down = gradients[:, hidden_cols:]
    next_moment_up, next_second_up, step_up = adam_update(grad_up, moment_up, second_up)
    next_moment_down, next_second_down, step_down = adam_update(grad_down, moment_down, second_down)
    local_rows = basis_up.shape[0]
    start_up = jnp.zeros((local_rows, hidden_cols), jnp.float32)
    start_down = jnp.zeros((hidden_cols, local_rows), jnp.float32)
    pieces = (
        lax.all_gather(step_up, "dp", axis=0, tiled=True),
        lax.all_gather(step_down, "dp", axis=0, tiled=True),
    )
    piece_rows = pieces[0].shape[0]
    cols_up = lax.slice_in_dim(basis_up, 0, piece_rows, axis=1)
    cols_down = lax.slice_in_dim(basis_down, 0, piece_rows, axis=1)
    delta_up = start_up + jnp.dot(cols_up, pieces[0], preferred_element_type=jnp.float32)
    delta_down = start_down + lax.dot_general(
        pieces[1], cols_down, (((0,), (1,)), ((), ())), preferred_element_type=jnp.float32
    )
    return (
        delta_up.astype(jnp.bfloat16),
        delta_down.astype(jnp.bfloat16),
        next_moment_up,
        next_second_up,
        next_moment_down,
        next_second_down,
    )


def solution(mesh):
    in_specs = (
        P("dp", None),
        P("dp", None),
        P("dp", "tensor"),
        P("dp", "tensor"),
        P("dp", None),
        P("dp", None),
        P("dp", "tensor"),
        P("dp", "tensor"),
        P("dp", "tensor"),
        P("dp", "tensor"),
    )
    out_specs = (
        P("dp", "tensor"),
        P("tensor", "dp"),
        P("dp", "tensor"),
        P("dp", "tensor"),
        P("dp", "tensor"),
        P("dp", "tensor"),
    )
    return jax.shard_map(local, mesh=mesh, in_specs=in_specs, out_specs=out_specs, check_vma=False)
```

profile of v0, /device:TPU:1, one launch (start us, length us, event | category | flops | bytes accessed | tf_op | source)
XLA Modules:
  0.0 620.8 jit_solution(680380413310168633)
XLA Ops:
  7.2 0.0 copy-start
  7.2 0.0 all-gather.5.cloned.1.call-start
  7.2 0.7 all-gather.5.cloned.1.call-update
  7.9 0.0 all-gather.7.cloned.1.call-start
  8.0 0.7 all-gather.7.cloned.1.call-update
  8.7 0.0 copy-start.1
  8.7 0.0 reduce-scatter.2.cloned.1.call-start
  8.7 103.6 %all-gather.5.cloned.1.call-done = bf16[8192,512]{1,0:T(8,128)(2,1)} async-done(((bf16[256,512]{1,0:T(8,128)(2,1)}), bf16[8192,512]{1,0:T(8,128)(2,1)}) %all-gather.5.cloned.1.call-update) | async-done | bytes 8388624 | tf_op jit(solution)/shard_map/all_gather | solution.py:39
  112.3 0.0 copy-done
  112.3 7.7 %convolution_convert_fusion.1 = bf16[512,3584]{1,0:T(8,128)(2,1)} fusion(bf16[128,3584]{1,0:T(8,128)(2,1)} %param.12, bf16[128,8192]{1,0:T(8,128)(2,1)S(1)} %copy-done, bf16[8192,512]{1,0:T(8,128)(2,1)} %all-gather.5.cloned.1.call-done), kind=kOutput, calls=%fused_computation.2 | convolution fusion | flops 1545404416 | bytes 15073280 | tf_op jit(solution)/shard_map/dot_general | solution.py:48
  120.0 90.3 %all-gather.7.cloned.1.call-done = bf16[8192,512]{1,0:T(8,128)(2,1)} async-done(((bf16[256,512]{1,0:T(8,128)(2,1)}), bf16[8192,512]{1,0:T(8,128)(2,1)}) %all-gather.7.cloned.1.call-update) | async-done | bytes 8388624 | tf_op jit(solution)/shard_map/all_gather | solution.py:40
  210.3 0.0 copy-done.1
  210.3 8.2 %convolution_convert_fusion = bf16[512,3584]{1,0:T(8,128)(2,1)} fusion(bf16[128,3584]{1,0:T(8,128)(2,1)S(1)} %copy-done.1, bf16[128,8192]{1,0:T(8,128)(2,1)} %param.11, bf16[8192,512]{1,0:T(8,128)(2,1)} %all-gather.7.cloned.1.call-done), kind=kOutput, calls=%fused_computation.1 | convolution fusion | flops 1545404416 | bytes 15073280 | tf_op jit(solution)/shard_map/dot_general | solution.py:51
  218.5 6.9 %pad_maximum_fusion = bf16[512,7168]{1,0:T(8,128)(2,1)} fusion(bf16[512,3584]{1,0:T(8,128)(2,1)} %convolution_convert_fusion, bf16[512,3584]{1,0:T(8,128)(2,1)} %convolution_convert_fusion.1), kind=kLoop, calls=%fused_computation | loop fusion | flops 14680064 | bytes 14680064 | tf_op jit(solution)/shard_map/concatenate | solution.py:55
  225.4 0.0 copy-start.4
  225.4 0.0 copy-start.5
  225.4 0.0 copy-start.6
  225.4 0.0 copy-start.7
  225.4 0.0 copy-start.2
  225.4 0.0 reduce-scatter.2.cloned.1.call-update
  225.5 0.0 all-gather.9.cloned.1.call-start
  225.5 221.0 %reduce-scatter.2.cloned.1.call-done = bf16[16,7168]{1,0:T(8,128)(2,1)} async-done(((bf16[512,7168]{1,0:T(8,128)(2,1)}), bf16[16,7168]{1,0:T(8,128)(2,1)}) %reduce-scatter.2.cloned.1.call-update) | async-done | bytes 229392 | tf_op jit(solution)/shard_map/reduce_scatter | solution.py:54
  446.6 1.0 convert_element_type.27
  447.5 0.0 copy-done.4
  447.5 0.0 copy-done.5
  447.6 0.0 copy-done.6
  447.6 0.0 copy-done.7
  447.6 1.2 divide_convert_fusion
  448.7 0.0 all-gather.9.cloned.1.call-update
  448.7 0.0 all-gather.11.cloned.1.call-start
  448.8 0.5 all-gather.11.cloned.1.call-update
  449.3 80.0 %all-gather.9.cloned.1.call-done = bf16[512,3584]{1,0:T(8,128)(2,1)} async-done(((bf16[16,3584]{1,0:T(8,128)(2,1)}), bf16[512,3584]{1,0:T(8,128)(2,1)}) %all-gather.9.cloned.1.call-update) | async-done | bytes 3670032 | tf_op jit(solution)/shard_map/all_gather | solution.py:68
  529.3 0.0 copy-done.2
  529.3 4.4 fusion
  533.8 0.0 copy-start.3
  533.8 3.8 copy.16
  537.6 72.3 %all-gather.11.cloned.1.call-done = bf16[512,3584]{1,0:T(8,128)(2,1)} async-done(((bf16[16,3584]{1,0:T(8,128)(2,1)}), bf16[512,3584]{1,0:T(8,128)(2,1)}) %all-gather.11.cloned.1.call-update) | async-done | bytes 3670032 | tf_op jit(solution)/shard_map/all_gather | solution.py:69
  609.9 0.0 copy-done.3
  609.9 4.4 convolution_convert_fusion.2
Async XLA Ops:
  7.2 105.1 %copy-start = (bf16[128,8192]{1,0:T(8,128)(2,1)S(1)}, bf16[128,8192]{1,0:T(8,128)(2,1)}, u32[]{:S(2)}) copy-start(bf16[128,8192]{1,0:T(8,128)(2,1)} %param.10) | copy-start | bytes 6291460
  7.2 105.1 %all-gather.5.cloned.1.call-start = ((), (), s32[]{:S(2)}) async-start(), calls=%async_computation.1 | async-start | bytes 8650752 | tf_op jit(solution)/shard_map/all_gather | solution.py:39
  7.9 202.4 %all-gather.7.cloned.1.call-start = ((), (), s32[]{:S(2)}) async-start(), calls=%async_computation.2 | async-start | bytes 8650752 | tf_op jit(solution)/shard_map/all_gather | solution.py:40
  8.7 201.6 %copy-start.1 = (bf16[128,3584]{1,0:T(8,128)(2,1)S(1)}, bf16[128,3584]{1,0:T(8,128)(2,1)}, u32[]{:S(2)}) copy-start(bf16[128,3584]{1,0:T(8,128)(2,1)} %param.13) | copy-start | bytes 2752516
  8.7 437.9 %reduce-scatter.2.cloned.1.call-start = ((), (), s32[]{:S(2)}) async-start(), calls=%async_computation.3 | async-start | bytes 7569408 | tf_op jit(solution)/shard_map/reduce_scatter | solution.py:54
  225.4 222.1 %copy-start.4 = (f32[16,3584]{1,0:T(8,128)S(1)}, f32[16,3584]{1,0:T(8,128)}, u32[]{:S(2)}) copy-start(f32[16,3584]{1,0:T(8,128)} %param.18) | copy-start | bytes 688132
  225.4 222.1 %copy-start.5 = (f32[16,3584]{1,0:T(8,128)S(1)}, f32[16,3584]{1,0:T(8,128)}, u32[]{:S(2)}) copy-start(f32[16,3584]{1,0:T(8,128)} %param.19) | copy-start | bytes 688132
  225.4 222.1 %copy-start.6 = (f32[16,3584]{1,0:T(8,128)S(1)}, f32[16,3584]{1,0:T(8,128)}, u32[]{:S(2)}) copy-start(f32[16,3584]{1,0:T(8,128)} %param.17) | copy-start | bytes 688132
  225.4 222.1 %copy-start.7 = (f32[16,3584]{1,0:T(8,128)S(1)}, f32[16,3584]{1,0:T(8,128)}, u32[]{:S(2)}) copy-start(f32[16,3584]{1,0:T(8,128)} %param.16) | copy-start | bytes 688132
  225.4 303.9 %copy-start.2 = (bf16[256,512]{1,0:T(8,128)(2,1)S(1)}, bf16[256,512]{1,0:T(8,128)(2,1)}, u32[]{:S(2)}) copy-start(bf16[256,512]{1,0:T(8,128)(2,1)} %param.14) | copy-start | bytes 786436
  225.5 303.9 %all-gather.9.cloned.1.call-start = ((), (), s32[]{:S(2)}) async-start(), calls=%async_computation.4 | async-start | bytes 3784704 | tf_op jit(solution)/shard_map/all_gather | solution.py:68
  448.7 161.1 %all-gather.11.cloned.1.call-start = ((), (), s32[]{:S(2)}) async-start(), calls=%async_computation.5 | async-start | bytes 3784704 | tf_op jit(solution)/shard_map/all_gather | solution.py:69
  533.8 76.1 %copy-start.3 = (bf16[256,512]{1,0:T(8,128)(2,1)S(1)}, bf16[256,512]{1,0:T(8,128)(2,1)}, u32[]{:S(2)}) copy-start(bf16[256,512]{1,0:T(8,128)(2,1)} %param.15) | copy-start | bytes 786436
Sparse Core Ops, SparseCore 0:
  10.6 101.6 all-gather.4
  114.9 95.3 all-gather.6
  225.6 220.9 reduce-scatter.1
  449.9 79.3 all-gather.8
  532.1 77.7 all-gather.10
where the time goes:
time: 623 us; the launch traced here: 621 us
  waiting for transfers between devices  569 us (91%)
  matrix products  24.8 us (4%)
  between operations  13.8 us (2%)
  other arithmetic  9 us (1%)
    reduce_scatter x1, waiting for transfers between devices, local(): lax.psum_scatter(jnp.concatenate([term_up, term_down], axis=1).astype(jnp...  221 us
    all_gather x1, waiting for transfers between devices, local(): lax.all_gather(basis_up, 'dp', axis=0, tiled=True)  104 us
    all_gather x1, waiting for transfers between devices, local(): lax.all_gather(basis_down, 'dp', axis=0, tiled=True)  90.3 us
    all_gather x1, waiting for transfers between devices, local(): lax.all_gather(step_up, 'dp', axis=0, tiled=True)  80 us
    all_gather x1, waiting for transfers between devices, local(): lax.all_gather(step_down, 'dp', axis=0, tiled=True)  72.3 us
  transfers between devices with their start and end apart: 5, of which 5 were waited for; matrix products, arithmetic and copies ran while one was open for 3% of the time, Pallas kernels for 0%

commit v1 on v0

v1 whole, which is shorter than its diff:
```python
import functools

import jax
import jax.numpy as jnp
from jax import lax
from jax.experimental import pallas as pl
from jax.experimental.pallas import tpu as pltpu
from jax.sharding import PartitionSpec as P

STEPS = 1000
momentum_decay = 0.9
square_decay = 0.999
adam_epsilon = 1e-08
update_scale = 2.5
first_fix = 1.0 - momentum_decay**STEPS
second_fix = 1.0 - square_decay**STEPS

MESH = pl.DeviceIdType.MESH
BF, F32 = jnp.bfloat16, jnp.float32

NX, NY, NZ = 4, 4, 8
TOK, D, R, FD = 128, 8192, 512, 3584
BR = D // (NX * NZ)
RY = R // NY
Q = FD // NX
OWN = R // (NX * NZ)
ZROWS = NX * OWN
W1 = 2048
TILE = 512
N_SEM = 256


def kernel(
    tokens,
    out_grad,
    up_grad,
    hidden,
    basis_up,
    basis_down,
    m_up,
    v_up,
    m_down,
    v_down,
    delta_up,
    delta_down,
    grads_out,
    t_buf,
    b_all,
    b_own,
    acc,
    u_buf,
    relay,
    pt,
    g_buf,
    rs_out,
    rs_in,
    gx,
    gr,
    mom,
    steps,
    d_up,
    d_down,
    ssem,
    rsem,
    lsem,
):
    dp, tn = lax.axis_index("dp"), lax.axis_index("tensor")
    x, z = lax.div(dp, NZ), lax.rem(dp, NZ)
    y, c = lax.div(tn, 2), lax.rem(tn, 2)

    def wrap(v, n):
        return lax.rem(v + n, n)

    def at(xo=0, zo=0, yo=0, co=0):
        return (
            wrap(x + xo, NX) * NZ + wrap(z + zo, NZ),
            wrap(y + yo, NY) * 2 + lax.rem(c + co, 2),
        )

    def x_dev(xx):
        return (xx * NZ + z, tn)

    used = [0]
    pending = []

    def send(src, dst, dev):
        k = used[0]
        used[0] += 1
        cp = pltpu.make_async_remote_copy(
            src_ref=src,
            dst_ref=dst,
            send_sem=ssem.at[k],
            recv_sem=rsem.at[k],
            device_id=dev,
            device_id_type=MESH,
        )
        cp.start()
        pending.append(cp)
        return cp

    local_used = [0]

    def load(src, dst):
        k = local_used[0]
        local_used[0] += 1
        cp = pltpu.make_async_copy(src, dst, lsem.at[k])
        cp.start()
        return cp

    def load_by_core(src0, src1, dst):
        k = local_used[0]
        local_used[0] += 1

        @pl.when(c == 0)
        def _():
            pltpu.make_async_copy(src0, dst, lsem.at[k]).start()

        @pl.when(c == 1)
        def _():
            pltpu.make_async_copy(src1, dst, lsem.at[k]).start()

        return pltpu.make_async_copy(src0, dst, lsem.at[k])

    def quarter(q):
        return pl.ds(pl.multiple_of(q * Q, 128), Q)

    def tok_rows(q):
        return pl.ds(pl.multiple_of(q * TOK, TOK), TOK)

    y_cols = pl.ds(pl.multiple_of(y * RY, RY), RY)

    b_reg0 = b_all.at[x, z]
    own_b = load_by_core(basis_up.at[:, y_cols], basis_down.at[:, y_cols], b_reg0)
    own_t = load_by_core(tokens, out_grad, t_buf)
    ins = (up_grad, hidden)
    own_u = [load(ins[m].at[:, quarter(x)], u_buf.at[m, tok_rows(x), :]) for m in (0, 1)]
    own_m = [load(r, mom.at[k]) for k, r in enumerate((m_up, v_up, m_down, v_down))]
    own_bases = [load(r, b_own.at[k]) for k, r in enumerate((basis_up, basis_down))]

    partners = [at(xo=k) for k in range(1, NX)]
    partners += [at(zo=1), at(zo=-1)]
    partners += [at(yo=k) for k in range(1, NY)]
    partners += [at(co=1)]
    barrier = pltpu.get_barrier_semaphore()
    for dev in partners:
        pl.semaphore_signal(barrier, inc=1, device_id=dev, device_id_type=MESH)
    acc[...] = jnp.zeros_like(acc)
    own_b.wait()
    pl.semaphore_wait(barrier, len(partners))

    dirs = (1, -1)

    def b_reg(xo, zo, half=None):
        ref = b_all.at[wrap(x + xo, NX), wrap(z + zo, NZ)]
        if half is None:
            return ref
        return ref.at[pl.ds(half * (BR // 2), BR // 2), :]

    def gather_xz(reg):
        hx, hz = {}, {}

        def z_first(xb):
            for d in dirs:
                blk = reg(xb, 0)
                hz[xb, d, 1] = send(blk, blk, at(zo=d))

        def z_step(xb, k):
            for d in dirs:
                hz[xb, d, k].wait_recv()
                if k < 4:
                    half = None if k < 3 else (0 if d > 0 else 1)
                    blk = reg(xb, -d * k, half)
                    hz[xb, d, k + 1] = send(blk, blk, at(zo=d))
            return [(xb, k), (xb, -k)] if k < 4 else [(xb, 4)]

        def r0():
            for d in dirs:
                blk = reg(0, 0)
                hx[d, 1] = send(blk, blk, at(xo=d))
            z_first(0)
            return [(0, 0)]

        def r1():
            for d in dirs:
                hx[d, 1].wait_recv()
                blk = reg(-d, 0, 0 if d > 0 else 1)
                hx[d, 2] = send(blk, blk, at(xo=d))
            z_first(-1)
            z_first(1)
            return [(-1, 0), (1, 0)]

        def r2():
            done = z_step(0, 1)
            for d in dirs:
                hx[d, 2].wait_recv()
            z_first(2)
            return done + [(2, 0)]

        def later(pairs):
            def run():
                done = []
                for xb, k in pairs:
                    done += z_step(xb, k)
                return done

            return run

        return [
            r0,
            r1,
            r2,
            later([(0, 2), (-1, 1), (1, 1)]),
            later([(0, 3), (-1, 2), (1, 2), (2, 1)]),
            later([(0, 4), (-1, 3), (1, 3), (2, 2)]),
            later([(-1, 4), (1, 4), (2, 3)]),
            later([(2, 4)]),
        ]

    def project(blocks):
        for xo, zo in blocks:
            xx, zz = wrap(x + xo, NX), wrap(z + zo, NZ)
            cols = pl.ds(pl.multiple_of((xx * NZ + zz) * BR, BR), BR)
            acc[...] += jnp.dot(t_buf[:, cols], b_all[xx, zz], preferred_element_type=F32)

    x1 = x + 1 - 2 * lax.rem(x, 2)
    x3 = NX - 1 - x
    x2 = lax.rem(x + 2, NX)
    near = ((x1, x3), (x3, x1))
    hu = {}
    rounds = gather_xz(b_reg)
    blocks = rounds[0]()
    for m in (0, 1):
        p1, p2 = near[m]
        hu[m, "b"] = send(ins[m].at[:, quarter(x2)], relay.at[m], x_dev(p1))
    for m in (0, 1):
        p1, p2 = near[m]
        hu[m, "a"] = send(ins[m].at[:, quarter(p1)], u_buf.at[m, tok_rows(x), :], x_dev(p1))
    for m in (0, 1):
        p1, p2 = near[m]
        hu[m, "c"] = send(ins[m].at[:, quarter(p2)], u_buf.at[m, tok_rows(x), :], x_dev(p2))
    own_t.wait()
    project(blocks)
    for k in range(1, len(rounds)):
        blocks = rounds[k]()
        if k == 4:
            for m in (0, 1):
                p1, p2 = near[m]
                hu[m, "b"].wait_recv()
                hu[m, "d"] = send(relay.at[m], u_buf.at[m, tok_rows(p1), :], x_dev(p2))
        project(blocks)

    def p_reg(xo, half=None):
        rows = pl.ds(0, R) if half is None else pl.ds(half * (R // 2), R // 2)
        return pt.at[c, rows, tok_rows(wrap(x + xo, NX))]

    mine = pt.at[c, y_cols, tok_rows(x)]
    mine[...] = acc[...].T.astype(BF)
    hp = [send(mine, mine, at(yo=k)) for k in range(1, NY)]
    for cp in hp:
        cp.wait_recv()
    hx = {}
    for d in dirs:
        hx[d, 1] = send(p_reg(0), p_reg(0), at(xo=d))
    hc = [send(p_reg(0), p_reg(0), at(co=1))]
    for d in dirs:
        hx[d, 1].wait_recv()
        blk = p_reg(-d, 0 if d > 0 else 1)
        hx[d, 2] = send(blk, blk, at(xo=d))
        hc.append(send(p_reg(-d), p_reg(-d), at(co=1)))
    for d in dirs:
        hx[d, 2].wait_recv()
        blk = p_reg(2, 0 if d > 0 else 1)
        hc.append(send(blk, blk, at(co=1)))
    for m in (0, 1):
        own_u[m].wait()
        for k in ("a", "c", "d"):
            hu[m, k].wait_recv()
    for cp in hc:
        cp.wait_recv()

    def gradient(m):
        for k in range(NX):
            part = jnp.dot(pt[m, k * 128 : (k + 1) * 128, :], u_buf[m], preferred_element_type=F32)
            g_buf[m, :, k * OWN : (k + 1) * OWN, :] = part.reshape(NZ, OWN, Q)

    hr = {}
    reach = {(0, 1): 3, (0, -1): 4, (1, 1): 4, (1, -1): 3}

    def rs_step(m, s):
        for j, d in enumerate(dirs):
            n = reach[m, d]
            if s >= n:
                continue
            val = g_buf[m, wrap(z + d * (n - s), NZ)]
            if s:
                hr[m, d, s - 1].wait_recv()
                val = val + rs_in[m, j, s - 1].astype(F32)
            rs_out[m, j, s] = val.astype(BF)
            hr[m, d, s] = send(rs_out.at[m, j, s], rs_in.at[m, j, s], at(zo=d))

    for m in (0, 1):
        gradient(m)
        rs_step(m, 0)
    for s in range(1, 4):
        for m in (0, 1):
            rs_step(m, s)

    hg = {}
    for m in (0, 1):
        val = g_buf[m, z]
        for j, d in enumerate(dirs):
            n = reach[m, d]
            hr[m, d, n - 1].wait_recv()
            val = val + rs_in[m, j, n - 1].astype(F32)
        gx[m] = val.astype(BF).reshape(NX, OWN, Q)
        gr[m, :, quarter(x)] = gx[m, x]
        for k in range(1, NX):
            xx = wrap(x + k, NX)
            hg[m, k] = send(gx.at[m, xx], gr.at[m, :, quarter(x)], x_dev(xx))

    for cp in own_m:
        cp.wait()

    own_rows = pl.ds(pl.multiple_of(dp * OWN, OWN), OWN)

    def adam(m):
        for k in range(1, NX):
            hg[m, k].wait_recv()

        @pl.loop(0, FD // TILE)
        def _(t):
            cols = pl.ds(pl.multiple_of(t * TILE, TILE), TILE)
            grad = gr[m, :, cols].astype(F32)
            moment = momentum_decay * mom[2 * m, :, cols] + (1.0 - momentum_decay) * grad
            second = square_decay * mom[2 * m + 1, :, cols] + (1.0 - square_decay) * grad * grad
            step = (
                update_scale
                * (moment * (1.0 / first_fix))
                / (jnp.sqrt(second * (1.0 / second_fix)) + adam_epsilon)
            )
            steps[m, own_rows, cols] = step.astype(BF)

    def s_reg(m, lo, hi):
        def reg(xo, zo, half=None):
            rows = (wrap(x + xo, NX) * NZ + wrap(z + zo, NZ)) * OWN
            width = hi - lo
            start = lo
            if half is not None:
                width //= 2
                start += half * width
            return steps.at[m, pl.ds(pl.multiple_of(rows, OWN), OWN), pl.ds(start, width)]

        return reg

    def gather_zx(reg):
        hz, hx = {}, {}

        def x_first(zo):
            for d in dirs:
                blk = reg(0, zo)
                hx[zo, d, 1] = send(blk, blk, at(xo=d))

        def x_relay(zo):
            for d in dirs:
                hx[zo, d, 1].wait_recv()
                blk = reg(-d, zo, 0 if d > 0 else 1)
                hx[zo, d, 2] = send(blk, blk, at(xo=d))

        def z_step(k):
            for d in dirs:
                hz[d, k].wait_recv()
                if k < 4:
                    blk = reg(0, -d * k, None if k < 3 else (0 if d > 0 else 1))
                    hz[d, k + 1] = send(blk, blk, at(zo=d))
            if k < 4:
                x_first(-k)
                x_first(k)
            else:
                x_first(4)

        def r0():
            for d in dirs:
                blk = reg(0, 0)
                hz[d, 1] = send(blk, blk, at(zo=d))
            x_first(0)

        def r1():
            z_step(1)
            x_relay(0)

        def r2():
            z_step(2)
            x_relay(-1)
            x_relay(1)

        def r3():
            z_step(3)

        def r4():
            z_step(4)
            x_relay(-2)
            x_relay(2)

        def r5():
            x_relay(-3)
            x_relay(3)

        def r6():
            x_relay(4)

        def r7():
            for zo in (0, -1, 1, -2, 2, -3, 3, 4):
                for d in dirs:
                    hx[zo, d, 2].wait_recv()

        return [r0, r1, r2, r3, r4, r5, r6, r7]

    plans = []
    for m in (0, 1):
        a, b = gather_zx(s_reg(m, 0, W1)), gather_xz(s_reg(m, W1, FD))
        plans.append((a, b))

    def run_round(m, k):
        a, b = plans[m]
        if k < len(b):
            b[k]()
        if k < len(a):
            a[k]()

    out_cps = []

    def update_up():
        @pl.loop(0, FD // TILE)
        def _(t):
            cols = pl.ds(pl.multiple_of(t * TILE, TILE), TILE)
            d_up[:, cols] = jnp.dot(b_own[0], steps[0, :, cols], preferred_element_type=F32).astype(BF)

    def update_down():
        @pl.loop(0, FD // TILE)
        def _(t):
            cols = pl.ds(pl.multiple_of(t * TILE, TILE), TILE)
            val = jnp.dot(b_own[1], steps[1, :, cols], preferred_element_type=F32)
            d_down[cols, :] = val.T.astype(BF)

    adam(0)
    run_round(0, 0)
    adam(1)
    n_rounds = 8
    for k in range(n_rounds):
        if k + 1 < n_rounds:
            run_round(0, k + 1)
        if k + 1 == n_rounds - 1:
            out_cps.append(load(gr, grads_out))
            for cp in own_bases:
                cp.wait()
            run_round(1, k)
            update_up()
            out_cps.append(load(d_up, delta_up))
        else:
            run_round(1, k)
    update_down()
    out_cps.append(load(d_down, delta_down))
    for cp in out_cps:
        cp.wait()
    for cp in pending:
        cp.wait_send()
    assert used[0] <= N_SEM, used[0]


def local(
    tokens_in,
    out_grad,
    up_grad,
    hidden_act,
    basis_up,
    basis_down,
    moment_up,
    second_up,
    moment_down,
    second_down,
):
    hbm = pl.BlockSpec(memory_space=pl.ANY)
    vmem = pltpu.VMEM
    delta_up, delta_down, grads = pl.pallas_call(
        kernel,
        out_shape=(
            jax.ShapeDtypeStruct((BR, FD), BF),
            jax.ShapeDtypeStruct((FD, BR), BF),
            jax.ShapeDtypeStruct((2, OWN, FD), BF),
        ),
        in_specs=[hbm] * 10,
        out_specs=(hbm, hbm, hbm),
        scratch_shapes=[
            vmem((TOK, D), BF),
            vmem((NX, NZ, BR, RY), BF),
            vmem((2, BR, R), BF),
            vmem((TOK, RY), F32),
            vmem((2, NX * TOK, Q), BF),
            vmem((2, TOK, Q), BF),
            vmem((2, R, NX * TOK), BF),
            vmem((2, NZ, ZROWS, Q), F32),
            vmem((2, 2, 4, ZROWS, Q), BF),
            vmem((2, 2, 4, ZROWS, Q), BF),
            vmem((2, NX, OWN, Q), BF),
            vmem((2, OWN, FD), BF),
            vmem((4, OWN, FD), F32),
            vmem((2, R, FD), BF),
            vmem((BR, FD), BF),
            vmem((FD, BR), BF),
            pltpu.SemaphoreType.DMA((N_SEM,)),
            pltpu.SemaphoreType.DMA((N_SEM,)),
            pltpu.SemaphoreType.DMA((16,)),
        ],
        compiler_params=pltpu.CompilerParams(
            collective_id=0, has_side_effects=True, vmem_limit_bytes=56 * 1024 * 1024
        ),
    )(
        tokens_in,
        out_grad,
        up_grad,
        hidden_act,
        basis_up,
        basis_down,
        moment_up,
        second_up,
        moment_down,
        second_down,
    )
    grads = grads.astype(F32)

    def moments(grad, moment, second):
        return (
            momentum_decay * moment + (1.0 - momentum_decay) * grad,
            square_decay * second + (1.0 - square_decay) * grad * grad,
        )

    next_moment_up, next_second_up = moments(grads[0], moment_up, second_up)
    next_moment_down, next_second_down = moments(grads[1], moment_down, second_down)
    return (delta_up, delta_down, next_moment_up, next_second_up, next_moment_down, next_second_down)


def solution(mesh):
    row, both = P("dp", None), P("dp", "tensor")
    return jax.shard_map(
        local,
        mesh=mesh,
        in_specs=(row, row, both, both, row, row, both, both, both, both),
        out_specs=(both, P("tensor", "dp"), both, both, both, both),
        check_vma=False,
    )
```

time: 623 us -> 147 us (0.24)
  waiting for transfers between devices: 569 us -> 0 us
  Pallas kernels: 0 us -> 138 us
  matrix products: 24.8 us -> 0 us
  between operations: 13.8 us -> 0.72 us
  other arithmetic: 9 us -> 2.08 us
    all_gather x4 -> x0, waiting for transfers between devices: 346 us -> none  [the longest x1 104 us: local(): lax.all_gather(basis_up, 'dp', axis=0, tiled=True)]
    reduce_scatter x1 -> x0, waiting for transfers between devices: 221 us -> none  [local(): lax.psum_scatter(jnp.concatenate([term_up, term_down], axis=1).astype(jnp...]
    pallas_call x0 -> x1, Pallas kernels: none -> 138 us  [local(): pl.pallas_call(kernel, out_shape=(jax.ShapeDtypeStruct((BR, FD), BF), jax...]
    dot_general x4 -> x0, matrix products: 24.8 us -> none  [the longest x1 8.23 us: local(): lax.dot_general(proj_grads, hidden_act, contract_rows, preferred_element_...]
    concatenate x1 -> x0, other arithmetic: 6.88 us -> none  [local(): jnp.concatenate([term_up, term_down], axis=1).astype(jnp.bfloat16)]
  transfers between devices with their start and end apart: 5 -> 0, of which waited for: 5 -> 0; matrix products, arithmetic and copies ran while one was open for 3% -> 0% of each run, Pallas kernels for 0% -> 0%
where the time goes in v1:
time: 147 us; the launch traced here: 145 us
  Pallas kernels  138 us (94%)
  local copies, waits for them, and re-layouts  3.41 us (2%)
  other arithmetic  2.08 us (1%)
    pallas_call x1, Pallas kernels, local(): pl.pallas_call(kernel, out_shape=(jax.ShapeDtypeStruct((BR, FD), BF), jax...  138 us
    unnamed x14, local copies, waits for them, and re-layouts  3.41 us

profile of v1, /device:TPU:1, one launch (start us, length us, event | category | flops | bytes accessed | tf_op | source)
XLA Modules:
  0.0 144.7 jit_solution(17579048790481981087)
XLA Ops:
  0.6 0.0 copy-start.2
  0.6 0.0 copy-start.3
  0.7 0.0 copy-start.4
  0.7 0.0 copy-start.5
  0.7 138.5 %shard_map.145 = (bf16[256,3584]{1,0:T(8,128)(2,1)}, bf16[3584,256]{1,0:T(8,128)(2,1)}, bf16[2,16,3584]{2,1,0:T(8,128)(2,1)}) custom-call(bf16[128,8192]{1,0:T(8,128)(2,1)} %tokens.1, bf16[128,8192]{1,0:T(8,128)(2,1)} %out_grad.1, bf16[128,3584]{1,0:T(8,128)(2,1)} %up_grad.1, bf16[128,3584]{1,0:T(8,128)(2,1)} %hidden.1, bf16[256,512]{1,0:T(8,128)(2,1)} %basis_up.1, ...), custom_call_target="tpu_custom_call" | custom-call | tf_op jit(solution)/shard_map/pallas_call | solution.py:484
  139.2 0.0 copy-start.1
  139.2 1.1 convert_element_type.3
  140.3 0.0 copy-done.2
  140.3 0.0 copy-done.3
  140.3 0.0 copy-done.4
  140.3 0.0 copy-done.5
  140.3 1.0 fusion.1
  141.3 0.0 copy-done.1
  141.3 0.0 copy-start
  141.3 1.2 copy.18
  142.5 0.9 copy-done
  143.4 1.2 copy.19
Async XLA Ops:
  0.6 139.6 %copy-start.2 = (f32[16,3584]{1,0:T(8,128)S(1)}, f32[16,3584]{1,0:T(8,128)}, u32[]{:S(2)}) copy-start(f32[16,3584]{1,0:T(8,128)} %m_up.1) | copy-start | bytes 688132
  0.6 139.6 %copy-start.3 = (f32[16,3584]{1,0:T(8,128)S(1)}, f32[16,3584]{1,0:T(8,128)}, u32[]{:S(2)}) copy-start(f32[16,3584]{1,0:T(8,128)} %v_up.1) | copy-start | bytes 688132
  0.7 139.6 %copy-start.4 = (f32[16,3584]{1,0:T(8,128)S(1)}, f32[16,3584]{1,0:T(8,128)}, u32[]{:S(2)}) copy-start(f32[16,3584]{1,0:T(8,128)} %m_down.1) | copy-start | bytes 688132
  0.7 139.6 %copy-start.5 = (f32[16,3584]{1,0:T(8,128)S(1)}, f32[16,3584]{1,0:T(8,128)}, u32[]{:S(2)}) copy-start(f32[16,3584]{1,0:T(8,128)} %v_down.1) | copy-start | bytes 688132
  139.2 2.1 %copy-start.1 = (bf16[256,3584]{1,0:T(8,128)(2,1)S(1)}, bf16[256,3584]{1,0:T(8,128)(2,1)}, u32[]{:S(2)}) copy-start(bf16[256,3584]{1,0:T(8,128)(2,1)} %get-tuple-element.22) | copy-start | bytes 5505028
  141.3 2.2 %copy-start = (bf16[3584,256]{1,0:T(8,128)(2,1)S(1)}, bf16[3584,256]{1,0:T(8,128)(2,1)}, u32[]{:S(2)}) copy-start(bf16[3584,256]{1,0:T(8,128)(2,1)} %get-tuple-element.23) | copy-start | bytes 5505028

commit v2 on v1

--- a/solution.py
+++ b/solution.py
@@ -41,9 +41,9 @@
     v_up,
     m_down,
     v_down,
-    delta_up,
-    delta_down,
-    grads_out,
+    d_up,
+    steps_down,
+    gr,
     t_buf,
     b_all,
     b_own,
@@ -55,11 +55,8 @@
     rs_out,
     rs_in,
     gx,
-    gr,
     mom,
-    steps,
-    d_up,
-    d_down,
+    steps_up,
     ssem,
     rsem,
     lsem,
@@ -83,20 +80,29 @@
     used = [0]
     pending = []
 
-    def send(src, dst, dev):
-        k = used[0]
-        used[0] += 1
-        cp = pltpu.make_async_remote_copy(
+    def take(n):
+        used[0] += n
+        return used[0] - n
+
+    def remote(src, dst, dev, k, rk):
+        return pltpu.make_async_remote_copy(
             src_ref=src,
             dst_ref=dst,
             send_sem=ssem.at[k],
-            recv_sem=rsem.at[k],
+            recv_sem=rsem.at[rk],
             device_id=dev,
             device_id_type=MESH,
         )
+
+    def send(src, dst, dev, k=None, rk=None):
+        k = take(1) if k is None else k
+        cp = remote(src, dst, dev, k, k if rk is None else rk)
         cp.start()
         pending.append(cp)
         return cp
+
+    def landed(ref, rk):
+        remote(ref, ref, at(co=1), 0, rk).wait_recv()
 
     local_used = [0]
 
@@ -133,14 +139,15 @@
     own_b = load_by_core(basis_up.at[:, y_cols], basis_down.at[:, y_cols], b_reg0)
     own_t = load_by_core(tokens, out_grad, t_buf)
     ins = (up_grad, hidden)
-    own_u = [load(ins[m].at[:, quarter(x)], u_buf.at[m, tok_rows(x), :]) for m in (0, 1)]
+    own_u = load_by_core(
+        up_grad.at[:, quarter(x)], hidden.at[:, quarter(x)], u_buf.at[c, tok_rows(x), :]
+    )
     own_m = [load(r, mom.at[k]) for k, r in enumerate((m_up, v_up, m_down, v_down))]
-    own_bases = [load(r, b_own.at[k]) for k, r in enumerate((basis_up, basis_down))]
-
-    partners = [at(xo=k) for k in range(1, NX)]
+    own_basis = load(basis_up, b_own)
+
+    partners = [at(xo=i, yo=j) for i in range(NX) for j in range(NY) if i or j]
+    partners += [at(xo=i, co=1) for i in range(NX)]
     partners += [at(zo=1), at(zo=-1)]
-    partners += [at(yo=k) for k in range(1, NY)]
-    partners += [at(co=1)]
     barrier = pltpu.get_barrier_semaphore()
     for dev in partners:
         pl.semaphore_signal(barrier, inc=1, device_id=dev, device_id_type=MESH)
@@ -156,7 +163,7 @@
             return ref
         return ref.at[pl.ds(half * (BR // 2), BR // 2), :]
 
-    def gather_xz(reg):
+    def gather_xz(reg, direct):
         hx, hz = {}, {}
 
         def z_first(xb):
@@ -174,25 +181,31 @@
             return [(xb, k), (xb, -k)] if k < 4 else [(xb, 4)]
 
         def r0():
-            for d in dirs:
-                blk = reg(0, 0)
+            blk = reg(0, 0)
+            for d in dirs:
                 hx[d, 1] = send(blk, blk, at(xo=d))
+            if direct:
+                hx[2] = send(blk, blk, at(xo=2))
             z_first(0)
             return [(0, 0)]
 
         def r1():
             for d in dirs:
                 hx[d, 1].wait_recv()
-                blk = reg(-d, 0, 0 if d > 0 else 1)
-                hx[d, 2] = send(blk, blk, at(xo=d))
+                if not direct:
+                    blk = reg(-d, 0, 0 if d > 0 else 1)
+                    hx[d, 2] = send(blk, blk, at(xo=d))
             z_first(-1)
             z_first(1)
             return [(-1, 0), (1, 0)]
 
         def r2():
             done = z_step(0, 1)
-            for d in dirs:
-                hx[d, 2].wait_recv()
+            if direct:
+                hx[2].wait_recv()
+            else:
+                for d in dirs:
+                    hx[d, 2].wait_recv()
             z_first(2)
             return done + [(2, 0)]
 
@@ -205,6 +218,16 @@
 
             return run
 
+        if direct:
+            return [
+                r0,
+                r1,
+                r2,
+                later([(-1, 1), (1, 1), (0, 2), (2, 1)]),
+                later([(-1, 2), (1, 2), (0, 3), (2, 2)]),
+                later([(-1, 3), (1, 3), (0, 4), (2, 3)]),
+                later([(-1, 4), (1, 4), (2, 4)]),
+            ]
         return [
             r0,
             r1,
@@ -226,61 +249,78 @@
     x3 = NX - 1 - x
     x2 = lax.rem(x + 2, NX)
     near = ((x1, x3), (x3, x1))
-    hu = {}
-    rounds = gather_xz(b_reg)
+    my_p1 = x1 + c * (x3 - x1)
+    my_p2 = x3 + c * (x1 - x3)
+
+    def core_dev(xx, m):
+        return (xx * NZ + z, y * 2 + m)
+
+    rounds = gather_xz(b_reg, True)
     blocks = rounds[0]()
+    got_b, got_a, got_c = take(2), take(2), take(2)
     for m in (0, 1):
         p1, p2 = near[m]
-        hu[m, "b"] = send(ins[m].at[:, quarter(x2)], relay.at[m], x_dev(p1))
+        send(ins[m].at[:, quarter(x2)], relay.at[c], core_dev(p1, m), rk=got_b + c)
     for m in (0, 1):
         p1, p2 = near[m]
-        hu[m, "a"] = send(ins[m].at[:, quarter(p1)], u_buf.at[m, tok_rows(x), :], x_dev(p1))
+        send(ins[m].at[:, quarter(p1)], u_buf.at[c, tok_rows(x), :], core_dev(p1, m), rk=got_a + c)
     for m in (0, 1):
         p1, p2 = near[m]
-        hu[m, "c"] = send(ins[m].at[:, quarter(p2)], u_buf.at[m, tok_rows(x), :], x_dev(p2))
+        send(ins[m].at[:, quarter(p2)], u_buf.at[c, tok_rows(x), :], core_dev(p2, m), rk=got_c + c)
+    k_own = take(1)
+    own_there = [
+        remote(ins[m].at[:, quarter(x)], u_buf.at[c, tok_rows(x), :], at(co=1), k_own, k_own)
+        for m in (0, 1)
+    ]
+
+    @pl.when(c == 1)
+    def _():
+        own_there[0].start()
+
+    @pl.when(c == 0)
+    def _():
+        own_there[1].start()
+
+    pending.append(own_there[0])
+    hd = []
     own_t.wait()
     project(blocks)
     for k in range(1, len(rounds)):
         blocks = rounds[k]()
         if k == 4:
-            for m in (0, 1):
-                p1, p2 = near[m]
-                hu[m, "b"].wait_recv()
-                hu[m, "d"] = send(relay.at[m], u_buf.at[m, tok_rows(p1), :], x_dev(p2))
+            for h in (0, 1):
+                landed(relay.at[h], got_b + h)
+                hd.append(send(relay.at[h], u_buf.at[h, tok_rows(my_p1), :], x_dev(my_p2)))
         project(blocks)
 
-    def p_reg(xo, half=None):
-        rows = pl.ds(0, R) if half is None else pl.ds(half * (R // 2), R // 2)
-        return pt.at[c, rows, tok_rows(wrap(x + xo, NX))]
-
-    mine = pt.at[c, y_cols, tok_rows(x)]
+    mine = pt.at[y_cols, tok_rows(x)]
     mine[...] = acc[...].T.astype(BF)
-    hp = [send(mine, mine, at(yo=k)) for k in range(1, NY)]
-    for cp in hp:
+    hp = {}
+    for xo in (0, 2, 1, -1):
+        for yo in range(NY):
+            if xo == 0 and yo == 0 or xo == 2 and yo > 1:
+                continue
+            hp[xo, yo] = send(mine, mine, at(xo=xo, yo=yo))
+    hp[1, 0].wait_recv()
+    hp[-1, 0].wait_recv()
+    for yo in (2, 3):
+        blk = pt.at[y_cols, tok_rows(wrap(x + 1, NX))]
+        hp[2, yo] = send(blk, blk, at(xo=-1, yo=yo))
+    own_u.wait()
+    landed(u_buf.at[1 - c, tok_rows(x), :], k_own)
+    for h in (0, 1):
+        landed(u_buf.at[h, tok_rows(my_p1), :], got_a + h)
+        landed(u_buf.at[h, tok_rows(my_p2), :], got_c + h)
+    for cp in hd:
         cp.wait_recv()
-    hx = {}
-    for d in dirs:
-        hx[d, 1] = send(p_reg(0), p_reg(0), at(xo=d))
-    hc = [send(p_reg(0), p_reg(0), at(co=1))]
-    for d in dirs:
-        hx[d, 1].wait_recv()
-        blk = p_reg(-d, 0 if d > 0 else 1)
-        hx[d, 2] = send(blk, blk, at(xo=d))
-        hc.append(send(p_reg(-d), p_reg(-d), at(co=1)))
-    for d in dirs:
-        hx[d, 2].wait_recv()
-        blk = p_reg(2, 0 if d > 0 else 1)
-        hc.append(send(blk, blk, at(co=1)))
-    for m in (0, 1):
-        own_u[m].wait()
-        for k in ("a", "c", "d"):
-            hu[m, k].wait_recv()
-    for cp in hc:
-        cp.wait_recv()
+    for key, cp in hp.items():
+        if key not in ((1, 0), (-1, 0)):
+            cp.wait_recv()
 
     def gradient(m):
         for k in range(NX):
-            part = jnp.dot(pt[m, k * 128 : (k + 1) * 128, :], u_buf[m], preferred_element_type=F32)
+            rows = pt[k * NZ * OWN : (k + 1) * NZ * OWN, :]
+            part = jnp.dot(rows, u_buf[m], preferred_element_type=F32)
             g_buf[m, :, k * OWN : (k + 1) * OWN, :] = part.reshape(NZ, OWN, Q)
 
     hr = {}
@@ -305,27 +345,31 @@
         for m in (0, 1):
             rs_step(m, s)
 
-    hg = {}
-    for m in (0, 1):
-        val = g_buf[m, z]
+    got_g = [take(2) for _ in range(1, NX)]
+    k_g = take(1)
+    for h in (0, 1):
+        val = g_buf[h, z]
         for j, d in enumerate(dirs):
-            n = reach[m, d]
-            hr[m, d, n - 1].wait_recv()
-            val = val + rs_in[m, j, n - 1].astype(F32)
-        gx[m] = val.astype(BF).reshape(NX, OWN, Q)
-        gr[m, :, quarter(x)] = gx[m, x]
+            n = reach[h, d]
+            hr[h, d, n - 1].wait_recv()
+            val = val + rs_in[h, j, n - 1].astype(F32)
+        gx[h] = val.astype(BF).reshape(NX, OWN, Q)
         for k in range(1, NX):
             xx = wrap(x + k, NX)
-            hg[m, k] = send(gx.at[m, xx], gr.at[m, :, quarter(x)], x_dev(xx))
+            send(gx.at[h, xx], gr.at[c, :, quarter(x)], core_dev(xx, h), rk=got_g[k - 1] + c)
+    gr[c, :, quarter(x)] = gx[c, x]
+    send(gx.at[1 - c, x], gr.at[c, :, quarter(x)], at(co=1), k=k_g)
 
     for cp in own_m:
         cp.wait()
+    landed(gr.at[1 - c, :, quarter(x)], k_g)
 
     own_rows = pl.ds(pl.multiple_of(dp * OWN, OWN), OWN)
+    steps = (steps_up, steps_down)
 
     def adam(m):
         for k in range(1, NX):
-            hg[m, k].wait_recv()
+            landed(gr.at[m, :, quarter(wrap(x - k, NX))], got_g[k - 1] + m)
 
         @pl.loop(0, FD // TILE)
         def _(t):
@@ -338,7 +382,7 @@
                 * (moment * (1.0 / first_fix))
                 / (jnp.sqrt(second * (1.0 / second_fix)) + adam_epsilon)
             )
-            steps[m, own_rows, cols] = step.astype(BF)
+            steps[m][own_rows, cols] = step.astype(BF)
 
     def s_reg(m, lo, hi):
         def reg(xo, zo, half=None):
@@ -348,7 +392,7 @@
             if half is not None:
                 width //= 2
                 start += half * width
-            return steps.at[m, pl.ds(pl.multiple_of(rows, OWN), OWN), pl.ds(start, width)]
+            return steps[m].at[pl.ds(pl.multiple_of(rows, OWN), OWN), pl.ds(start, width)]
 
         return reg
 
@@ -417,7 +461,7 @@
 
     plans = []
     for m in (0, 1):
-        a, b = gather_zx(s_reg(m, 0, W1)), gather_xz(s_reg(m, W1, FD))
+        a, b = gather_zx(s_reg(m, 0, W1)), gather_xz(s_reg(m, W1, FD), False)
         plans.append((a, b))
 
     def run_round(m, k):
@@ -427,20 +471,11 @@
         if k < len(a):
             a[k]()
 
-    out_cps = []
-
     def update_up():
         @pl.loop(0, FD // TILE)
         def _(t):
             cols = pl.ds(pl.multiple_of(t * TILE, TILE), TILE)
-            d_up[:, cols] = jnp.dot(b_own[0], steps[0, :, cols], preferred_element_type=F32).astype(BF)
-
-    def update_down():
-        @pl.loop(0, FD // TILE)
-        def _(t):
-            cols = pl.ds(pl.multiple_of(t * TILE, TILE), TILE)
-            val = jnp.dot(b_own[1], steps[1, :, cols], preferred_element_type=F32)
-            d_down[cols, :] = val.T.astype(BF)
+            d_up[:, cols] = jnp.dot(b_own[...], steps_up[:, cols], preferred_element_type=F32).astype(BF)
 
     adam(0)
     run_round(0, 0)
@@ -449,22 +484,57 @@
     for k in range(n_rounds):
         if k + 1 < n_rounds:
             run_round(0, k + 1)
+        run_round(1, k)
         if k + 1 == n_rounds - 1:
-            out_cps.append(load(gr, grads_out))
-            for cp in own_bases:
-                cp.wait()
-            run_round(1, k)
+            own_basis.wait()
             update_up()
-            out_cps.append(load(d_up, delta_up))
-        else:
-            run_round(1, k)
-    update_down()
-    out_cps.append(load(d_down, delta_down))
-    for cp in out_cps:
-        cp.wait()
     for cp in pending:
         cp.wait_send()
     assert used[0] <= N_SEM, used[0]
+
+
+def finish(
+    d_up,
+    steps_down,
+    gr,
+    basis_down,
+    m_up,
+    v_up,
+    m_down,
+    v_down,
+    delta_up,
+    delta_down,
+    next_m_up,
+    next_v_up,
+    next_m_down,
+    next_v_down,
+    d_down,
+    new,
+    sem,
+):
+    cps = []
+
+    def store(src, dst):
+        cp = pltpu.make_async_copy(src, dst, sem.at[len(cps)])
+        cp.start()
+        cps.append(cp)
+
+    store(d_up, delta_up)
+    old = ((m_up, v_up), (m_down, v_down))
+    outs = ((next_m_up, next_v_up), (next_m_down, next_v_down))
+    for k in (0, 1):
+        grad = gr[k].astype(F32)
+        new[k, 0] = momentum_decay * old[k][0][...] + (1.0 - momentum_decay) * grad
+        new[k, 1] = square_decay * old[k][1][...] + (1.0 - square_decay) * grad * grad
+        for j in (0, 1):
+            store(new.at[k, j], outs[k][j])
+    for t in range(FD // TILE):
+        rows = pl.ds(t * TILE, TILE)
+        val = jnp.dot(basis_down[...], steps_down[:, rows], preferred_element_type=F32)
+        d_down[rows, :] = val.T.astype(BF)
+        store(d_down.at[rows, :], delta_down.at[rows, :])
+    for cp in cps:
+        cp.wait()
 
 
 def local(
@@ -480,63 +550,57 @@
     second_down,
 ):
     hbm = pl.BlockSpec(memory_space=pl.ANY)
+    in_vmem = pl.BlockSpec(memory_space=pltpu.VMEM)
     vmem = pltpu.VMEM
-    delta_up, delta_down, grads = pl.pallas_call(
+    moments = (moment_up, second_up, moment_down, second_down)
+    operands = (tokens_in, out_grad, up_grad, hidden_act, basis_up, basis_down, *moments)
+    d_up, steps_down, grads = pl.pallas_call(
         kernel,
-        out_shape=(
-            jax.ShapeDtypeStruct((BR, FD), BF),
-            jax.ShapeDtypeStruct((FD, BR), BF),
-            jax.ShapeDtypeStruct((2, OWN, FD), BF),
-        ),
+        out_shape=(vmem((BR, FD), BF), vmem((R, FD), BF), vmem((2, OWN, FD), BF)),
         in_specs=[hbm] * 10,
-        out_specs=(hbm, hbm, hbm),
+        out_specs=(in_vmem, in_vmem, in_vmem),
         scratch_shapes=[
             vmem((TOK, D), BF),
             vmem((NX, NZ, BR, RY), BF),
-            vmem((2, BR, R), BF),
+            vmem((BR, R), BF),
             vmem((TOK, RY), F32),
             vmem((2, NX * TOK, Q), BF),
             vmem((2, TOK, Q), BF),
-            vmem((2, R, NX * TOK), BF),
+            vmem((R, NX * TOK), BF),
             vmem((2, NZ, ZROWS, Q), F32),
             vmem((2, 2, 4, ZROWS, Q), BF),
             vmem((2, 2, 4, ZROWS, Q), BF),
             vmem((2, NX, OWN, Q), BF),
-            vmem((2, OWN, FD), BF),
             vmem((4, OWN, FD), F32),
-            vmem((2, R, FD), BF),
-            vmem((BR, FD), BF),
-            vmem((FD, BR), BF),
+            vmem((R, FD), BF),
             pltpu.SemaphoreType.DMA((N_SEM,)),
             pltpu.SemaphoreType.DMA((N_SEM,)),
             pltpu.SemaphoreType.DMA((16,)),
         ],
         compiler_params=pltpu.CompilerParams(
-            collective_id=0, has_side_effects=True, vmem_limit_bytes=56 * 1024 * 1024
+            collective_id=0, has_side_effects=True, vmem_limit_bytes=36 * 1024 * 1024
         ),
-    )(
-        tokens_in,
-        out_grad,
-        up_grad,
-        hidden_act,
-        basis_up,
-        basis_down,
-        moment_up,
-        second_up,
-        moment_down,
-        second_down,
-    )
-    grads = grads.astype(F32)
-
-    def moments(grad, moment, second):
-        return (
-            momentum_decay * moment + (1.0 - momentum_decay) * grad,
-            square_decay * second + (1.0 - square_decay) * grad * grad,
-        )
-
-    next_moment_up, next_second_up = moments(grads[0], moment_up, second_up)
-    next_moment_down, next_second_down = moments(grads[1], moment_down, second_down)
-    return (delta_up, delta_down, next_moment_up, next_second_up, next_moment_down, next_second_down)
+    )(*(pltpu.with_memory_space_constraint(v, pltpu.HBM) for v in operands))
+    small = jax.ShapeDtypeStruct((OWN, FD), F32)
+    return pl.pallas_call(
+        finish,
+        out_shape=(
+            jax.ShapeDtypeStruct((BR, FD), BF),
+            jax.ShapeDtypeStruct((FD, BR), BF),
+            small,
+            small,
+            small,
+            small,
+        ),
+        in_specs=[in_vmem] * 8,
+        out_specs=(hbm,) * 6,
+        scratch_shapes=[
+            vmem((FD, BR), BF),
+            vmem((2, 2, OWN, FD), F32),
+            pltpu.SemaphoreType.DMA((5 + FD // TILE,)),
+        ],
+        compiler_params=pltpu.CompilerParams(vmem_limit_bytes=16 * 1024 * 1024),
+    )(d_up, steps_down, grads, basis_down, *moments)
 
 
 def solution(mesh):

time: 147 us -> 123 us (0.84); the launches traced: 145 us -> 123 us
  Pallas kernels: 138 us -> 122 us
  local copies, waits for them, and re-layouts: 3.41 us -> 0.02 us
  other arithmetic: 2.08 us -> 0 us
    pallas_call x1 -> x2, Pallas kernels: 138 us -> 122 us  [the longest x1 119 us: local(): pl.pallas_call(kernel, out_shape=(vmem((BR, FD), BF), vmem((R, FD), BF),...]
    unnamed x14 -> x10, local copies, waits for them, and re-layouts: 3.41 us -> 0.02 us
where the time goes in v2:
time: 123 us
  Pallas kernels  122 us (99%)
    pallas_call x1, Pallas kernels, local(): pl.pallas_call(kernel, out_shape=(vmem((BR, FD), BF), vmem((R, FD), BF),...  119 us
    pallas_call x1, Pallas kernels, local(): pl.pallas_call(finish, out_shape=(jax.ShapeDtypeStruct((BR, FD), BF), jax...  2.49 us

profile of v2, /device:TPU:1, one launch (start us, length us, event | category | flops | bytes accessed | tf_op | source)
XLA Modules:
  0.0 122.6 jit_solution(14673392120294076573)
XLA Ops:
  0.6 0.0 copy-start.4
  0.6 0.0 copy-start.3
  0.7 0.0 copy-start.2
  0.7 0.0 copy-start.1
  0.7 0.0 copy-start
  0.7 119.4 %shard_map.145 = (bf16[256,3584]{1,0:T(8,128)(2,1)S(1)}, bf16[512,3584]{1,0:T(8,128)(2,1)S(1)}, bf16[2,16,3584]{2,1,0:T(8,128)(2,1)S(1)}) custom-call(bf16[128,8192]{1,0:T(8,128)(2,1)} %tokens.1, bf16[128,8192]{1,0:T(8,128)(2,1)} %out_grad.1, bf16[128,3584]{1,0:T(8,128)(2,1)} %up_grad.1, bf16[128,3584]{1,0:T(8,128)(2,1)} %hidden.1, ...), custom_call_target="tpu_custom_call" | custom-call | tf_op jit(solution)/shard_map/pallas_call | solution.py:557
  120.1 0.0 copy-done.4
  120.1 0.0 copy-done.3
  120.1 0.0 copy-done.2
  120.1 0.0 copy-done.1
  120.1 0.0 copy-done
  120.1 2.5 %shard_map.146 = (bf16[256,3584]{1,0:T(8,128)(2,1)}, bf16[3584,256]{1,0:T(8,128)(2,1)}, f32[16,3584]{1,0:T(8,128)}, f32[16,3584]{1,0:T(8,128)}, f32[16,3584]{1,0:T(8,128)}, /*index=5*/f32[16,3584]{1,0:T(8,128)}) custom-call(bf16[256,3584]{1,0:T(8,128)(2,1)S(1)} %get-tuple-element.9.d_up, bf16[512,3584]{1,0:T(8,128)(2,1)S(1)} %get-tuple-element.10.steps_down, ...), custom_call_target="tpu_custom_call" | custom-call | tf_op jit(solution)/shard_map/pallas_call | solution.py:585
Async XLA Ops:
  0.6 119.4 %copy-start.4 = (f32[16,3584]{1,0:T(8,128)S(1)}, f32[16,3584]{1,0:T(8,128)}, u32[]{:S(2)}) copy-start(f32[16,3584]{1,0:T(8,128)} %v_down.3) | copy-start | bytes 688132
  0.6 119.4 %copy-start.3 = (f32[16,3584]{1,0:T(8,128)S(1)}, f32[16,3584]{1,0:T(8,128)}, u32[]{:S(2)}) copy-start(f32[16,3584]{1,0:T(8,128)} %m_down.3) | copy-start | bytes 688132
  0.7 119.4 %copy-start.2 = (f32[16,3584]{1,0:T(8,128)S(1)}, f32[16,3584]{1,0:T(8,128)}, u32[]{:S(2)}) copy-start(f32[16,3584]{1,0:T(8,128)} %v_up.3) | copy-start | bytes 688132
  0.7 119.4 %copy-start.1 = (f32[16,3584]{1,0:T(8,128)S(1)}, f32[16,3584]{1,0:T(8,128)}, u32[]{:S(2)}) copy-start(f32[16,3584]{1,0:T(8,128)} %m_up.3) | copy-start | bytes 688132
  0.7 119.4 %copy-start = (bf16[256,512]{1,0:T(8,128)(2,1)S(1)}, bf16[256,512]{1,0:T(8,128)(2,1)}, u32[]{:S(2)}) copy-start(bf16[256,512]{1,0:T(8,128)(2,1)} %basis_down.3) | copy-start | bytes 786436

commit v3 on v2

--- a/solution.py
+++ b/solution.py
@@ -25,9 +25,11 @@
 Q = FD // NX
 OWN = R // (NX * NZ)
 ZROWS = NX * OWN
-W1 = 2048
+QS, QO = (512, 384), (0, 512)
+FS = tuple(NX * w for w in QS)
+W1 = (1280, 896)
 TILE = 512
-N_SEM = 256
+N_SEM = 320
 
 
 def kernel(
@@ -41,9 +43,11 @@
     v_up,
     m_down,
     v_down,
+    steps1,
     d_up,
-    steps_down,
-    gr,
+    d_down,
+    gr0,
+    gr1,
     t_buf,
     b_all,
     b_own,
@@ -52,11 +56,14 @@
     relay,
     pt,
     g_buf,
-    rs_out,
-    rs_in,
-    gx,
+    rs_out0,
+    rs_out1,
+    rs_in0,
+    rs_in1,
+    gx0,
+    gx1,
     mom,
-    steps_up,
+    steps0,
     ssem,
     rsem,
     lsem,
@@ -142,8 +149,8 @@
     own_u = load_by_core(
         up_grad.at[:, quarter(x)], hidden.at[:, quarter(x)], u_buf.at[c, tok_rows(x), :]
     )
+    own_bases = [load(r, b_own.at[k]) for k, r in enumerate((basis_up, basis_down))]
     own_m = [load(r, mom.at[k]) for k, r in enumerate((m_up, v_up, m_down, v_down))]
-    own_basis = load(basis_up, b_own)
 
     partners = [at(xo=i, yo=j) for i in range(NX) for j in range(NY) if i or j]
     partners += [at(xo=i, co=1) for i in range(NX)]
@@ -317,84 +324,71 @@
         if key not in ((1, 0), (-1, 0)):
             cp.wait_recv()
 
-    def gradient(m):
+    def cols_of(st):
+        return pl.ds(QO[st], QS[st])
+
+    def gradient(st, h):
         for k in range(NX):
             rows = pt[k * NZ * OWN : (k + 1) * NZ * OWN, :]
-            part = jnp.dot(rows, u_buf[m], preferred_element_type=F32)
-            g_buf[m, :, k * OWN : (k + 1) * OWN, :] = part.reshape(NZ, OWN, Q)
-
+            part = jnp.dot(rows, u_buf[h, :, cols_of(st)], preferred_element_type=F32)
+            g_buf[h, :, k * OWN : (k + 1) * OWN, cols_of(st)] = part.reshape(NZ, OWN, QS[st])
+
+    rs_out, rs_in, gx, gr, steps = (rs_out0, rs_out1), (rs_in0, rs_in1), (gx0, gx1), (gr0, gr1), (steps0, steps1)
     hr = {}
     reach = {(0, 1): 3, (0, -1): 4, (1, 1): 4, (1, -1): 3}
 
-    def rs_step(m, s):
+    def rs_step(st, h, s):
         for j, d in enumerate(dirs):
-            n = reach[m, d]
+            n = reach[h, d]
             if s >= n:
                 continue
-            val = g_buf[m, wrap(z + d * (n - s), NZ)]
+            val = g_buf[h, wrap(z + d * (n - s), NZ), :, cols_of(st)]
             if s:
-                hr[m, d, s - 1].wait_recv()
-                val = val + rs_in[m, j, s - 1].astype(F32)
-            rs_out[m, j, s] = val.astype(BF)
-            hr[m, d, s] = send(rs_out.at[m, j, s], rs_in.at[m, j, s], at(zo=d))
-
-    for m in (0, 1):
-        gradient(m)
-        rs_step(m, 0)
-    for s in range(1, 4):
+                hr[st, h, d, s - 1].wait_recv()
+                val = val + rs_in[st][h, j, s - 1].astype(F32)
+            rs_out[st][h, j, s] = val.astype(BF)
+            hr[st, h, d, s] = send(rs_out[st].at[h, j, s], rs_in[st].at[h, j, s], at(zo=d))
+
+    got_g = [[take(2) for _ in range(1, NX)] for st in (0, 1)]
+    k_g = [take(1) for st in (0, 1)]
+
+    def place(st, q):
+        return pl.ds(pl.multiple_of(q * QS[st], 128), QS[st])
+
+    def to_owners(st):
+        for h in (0, 1):
+            val = g_buf[h, z, :, cols_of(st)]
+            for j, d in enumerate(dirs):
+                n = reach[h, d]
+                hr[st, h, d, n - 1].wait_recv()
+                val = val + rs_in[st][h, j, n - 1].astype(F32)
+            gx[st][h] = val.astype(BF).reshape(NX, OWN, QS[st])
+            for k in range(1, NX):
+                xx = wrap(x + k, NX)
+                dst = gr[st].at[c, :, place(st, x)]
+                send(gx[st].at[h, xx], dst, core_dev(xx, h), rk=got_g[st][k - 1] + c)
+        gr[st][c, :, place(st, x)] = gx[st][c, x]
+        send(gx[st].at[1 - c, x], gr[st].at[c, :, place(st, x)], at(co=1), k=k_g[st])
+
+    own_rows = pl.ds(pl.multiple_of(dp * OWN, OWN), OWN)
+
+    def adam(st):
+        landed(gr[st].at[1 - c, :, place(st, x)], k_g[st])
         for m in (0, 1):
-            rs_step(m, s)
-
-    got_g = [take(2) for _ in range(1, NX)]
-    k_g = take(1)
-    for h in (0, 1):
-        val = g_buf[h, z]
-        for j, d in enumerate(dirs):
-            n = reach[h, d]
-            hr[h, d, n - 1].wait_recv()
-            val = val + rs_in[h, j, n - 1].astype(F32)
-        gx[h] = val.astype(BF).reshape(NX, OWN, Q)
-        for k in range(1, NX):
-            xx = wrap(x + k, NX)
-            send(gx.at[h, xx], gr.at[c, :, quarter(x)], core_dev(xx, h), rk=got_g[k - 1] + c)
-    gr[c, :, quarter(x)] = gx[c, x]
-    send(gx.at[1 - c, x], gr.at[c, :, quarter(x)], at(co=1), k=k_g)
-
-    for cp in own_m:
-        cp.wait()
-    landed(gr.at[1 - c, :, quarter(x)], k_g)
-
-    own_rows = pl.ds(pl.multiple_of(dp * OWN, OWN), OWN)
-    steps = (steps_up, steps_down)
-
-    def adam(m):
-        for k in range(1, NX):
-            landed(gr.at[m, :, quarter(wrap(x - k, NX))], got_g[k - 1] + m)
-
-        @pl.loop(0, FD // TILE)
-        def _(t):
-            cols = pl.ds(pl.multiple_of(t * TILE, TILE), TILE)
-            grad = gr[m, :, cols].astype(F32)
-            moment = momentum_decay * mom[2 * m, :, cols] + (1.0 - momentum_decay) * grad
-            second = square_decay * mom[2 * m + 1, :, cols] + (1.0 - square_decay) * grad * grad
-            step = (
-                update_scale
-                * (moment * (1.0 / first_fix))
-                / (jnp.sqrt(second * (1.0 / second_fix)) + adam_epsilon)
-            )
-            steps[m][own_rows, cols] = step.astype(BF)
-
-    def s_reg(m, lo, hi):
-        def reg(xo, zo, half=None):
-            rows = (wrap(x + xo, NX) * NZ + wrap(z + zo, NZ)) * OWN
-            width = hi - lo
-            start = lo
-            if half is not None:
-                width //= 2
-                start += half * width
-            return steps[m].at[pl.ds(pl.multiple_of(rows, OWN), OWN), pl.ds(start, width)]
-
-        return reg
+            for k in range(1, NX):
+                landed(gr[st].at[m, :, place(st, wrap(x - k, NX))], got_g[st][k - 1] + m)
+            for q in range(NX):
+                cols = pl.ds(q * Q + QO[st], QS[st])
+                here = pl.ds(q * QS[st], QS[st])
+                grad = gr[st][m, :, here].astype(F32)
+                moment = momentum_decay * mom[2 * m, :, cols] + (1.0 - momentum_decay) * grad
+                second = square_decay * mom[2 * m + 1, :, cols] + (1.0 - square_decay) * grad * grad
+                step = (
+                    update_scale
+                    * (moment * (1.0 / first_fix))
+                    / (jnp.sqrt(second * (1.0 / second_fix)) + adam_epsilon)
+                )
+                steps[st][m, own_rows, here] = step.astype(BF)
 
     def gather_zx(reg):
         hz, hx = {}, {}
@@ -459,44 +453,65 @@
 
         return [r0, r1, r2, r3, r4, r5, r6, r7]
 
-    plans = []
-    for m in (0, 1):
-        a, b = gather_zx(s_reg(m, 0, W1)), gather_xz(s_reg(m, W1, FD), False)
-        plans.append((a, b))
-
-    def run_round(m, k):
-        a, b = plans[m]
-        if k < len(b):
-            b[k]()
-        if k < len(a):
-            a[k]()
-
-    def update_up():
-        @pl.loop(0, FD // TILE)
-        def _(t):
-            cols = pl.ds(pl.multiple_of(t * TILE, TILE), TILE)
-            d_up[:, cols] = jnp.dot(b_own[...], steps_up[:, cols], preferred_element_type=F32).astype(BF)
-
+    def s_reg(st, lo, hi):
+        def reg(xo, zo, half=None):
+            rows = (wrap(x + xo, NX) * NZ + wrap(z + zo, NZ)) * OWN
+            rows = pl.ds(pl.multiple_of(rows, OWN), OWN)
+            return steps[st].at[slice(None) if half is None else half, rows, lo:hi]
+
+        return reg
+
+    plans = [
+        (gather_xz(s_reg(st, W1[st], FS[st]), False), gather_zx(s_reg(st, 0, W1[st])))
+        for st in (0, 1)
+    ]
+
+    def run_round(st, k):
+        for plan in plans[st]:
+            plan[k]()
+
+    def update():
+        for t in range(FS[0] // TILE):
+            cols = pl.ds(t * TILE, TILE)
+            val = jnp.dot(b_own[0], steps0[0, :, cols], preferred_element_type=F32)
+            d_up[:, cols] = val.astype(BF)
+            val = jnp.dot(b_own[1], steps0[1, :, cols], preferred_element_type=F32)
+            d_down[cols, :] = val.T.astype(BF)
+
+    for st in (0, 1):
+        for h in (0, 1):
+            gradient(st, h)
+            rs_step(st, h, 0)
+    for k in range(1, 4):
+        for st in (0, 1):
+            for h in (0, 1):
+                rs_step(st, h, k)
+    to_owners(0)
+    to_owners(1)
+    for cp in own_m + own_bases:
+        cp.wait()
     adam(0)
     run_round(0, 0)
     adam(1)
-    n_rounds = 8
-    for k in range(n_rounds):
-        if k + 1 < n_rounds:
-            run_round(0, k + 1)
+    run_round(1, 0)
+    for k in range(1, 7):
+        run_round(0, k)
         run_round(1, k)
-        if k + 1 == n_rounds - 1:
-            own_basis.wait()
-            update_up()
+    run_round(0, 7)
+    update()
+    run_round(1, 7)
     for cp in pending:
         cp.wait_send()
     assert used[0] <= N_SEM, used[0]
 
 
 def finish(
-    d_up,
-    steps_down,
-    gr,
+    steps1,
+    d_up0,
+    d_down0,
+    gr0,
+    gr1,
+    basis_up,
     basis_down,
     m_up,
     v_up,
@@ -508,6 +523,7 @@
     next_v_up,
     next_m_down,
     next_v_down,
+    d_up,
     d_down,
     new,
     sem,
@@ -519,20 +535,33 @@
         cp.start()
         cps.append(cp)
 
-    store(d_up, delta_up)
+    def places(st, q):
+        return pl.ds(q * QS[st], QS[st]), pl.ds(q * Q + QO[st], QS[st])
+
+    for q in range(NX):
+        here, there = places(0, q)
+        store(d_up0.at[:, here], delta_up.at[:, there])
+        store(d_down0.at[here, :], delta_down.at[there, :])
     old = ((m_up, v_up), (m_down, v_down))
     outs = ((next_m_up, next_v_up), (next_m_down, next_v_down))
     for k in (0, 1):
-        grad = gr[k].astype(F32)
-        new[k, 0] = momentum_decay * old[k][0][...] + (1.0 - momentum_decay) * grad
-        new[k, 1] = square_decay * old[k][1][...] + (1.0 - square_decay) * grad * grad
+        for st, gr in enumerate((gr0, gr1)):
+            for q in range(NX):
+                here, there = places(st, q)
+                grad = gr[k, :, here].astype(F32)
+                moment, second = old[k][0][:, there], old[k][1][:, there]
+                new[k, 0, :, there] = momentum_decay * moment + (1.0 - momentum_decay) * grad
+                new[k, 1, :, there] = square_decay * second + (1.0 - square_decay) * grad * grad
         for j in (0, 1):
             store(new.at[k, j], outs[k][j])
-    for t in range(FD // TILE):
-        rows = pl.ds(t * TILE, TILE)
-        val = jnp.dot(basis_down[...], steps_down[:, rows], preferred_element_type=F32)
-        d_down[rows, :] = val.T.astype(BF)
-        store(d_down.at[rows, :], delta_down.at[rows, :])
+    for q in range(NX):
+        here, there = places(1, q)
+        val = jnp.dot(basis_down[...], steps1[1, :, here], preferred_element_type=F32)
+        d_down[here, :] = val.T.astype(BF)
+        store(d_down.at[here, :], delta_down.at[there, :])
+        val = jnp.dot(basis_up[...], steps1[0, :, here], preferred_element_type=F32)
+        d_up[:, here] = val.astype(BF)
+        store(d_up.at[:, here], delta_up.at[:, there])
     for cp in cps:
         cp.wait()
 
@@ -554,31 +583,40 @@
     vmem = pltpu.VMEM
     moments = (moment_up, second_up, moment_down, second_down)
     operands = (tokens_in, out_grad, up_grad, hidden_act, basis_up, basis_down, *moments)
-    d_up, steps_down, grads = pl.pallas_call(
+    kept = pl.pallas_call(
         kernel,
-        out_shape=(vmem((BR, FD), BF), vmem((R, FD), BF), vmem((2, OWN, FD), BF)),
+        out_shape=(
+            vmem((2, R, FS[1]), BF),
+            vmem((BR, FS[0]), BF),
+            vmem((FS[0], BR), BF),
+            vmem((2, OWN, FS[0]), BF),
+            vmem((2, OWN, FS[1]), BF),
+        ),
         in_specs=[hbm] * 10,
-        out_specs=(in_vmem, in_vmem, in_vmem),
+        out_specs=(in_vmem,) * 5,
         scratch_shapes=[
             vmem((TOK, D), BF),
             vmem((NX, NZ, BR, RY), BF),
-            vmem((BR, R), BF),
+            vmem((2, BR, R), BF),
             vmem((TOK, RY), F32),
             vmem((2, NX * TOK, Q), BF),
             vmem((2, TOK, Q), BF),
             vmem((R, NX * TOK), BF),
             vmem((2, NZ, ZROWS, Q), F32),
-            vmem((2, 2, 4, ZROWS, Q), BF),
-            vmem((2, 2, 4, ZROWS, Q), BF),
-            vmem((2, NX, OWN, Q), BF),
+            vmem((2, 2, 4, ZROWS, QS[0]), BF),
+            vmem((2, 2, 4, ZROWS, QS[1]), BF),
+            vmem((2, 2, 4, ZROWS, QS[0]), BF),
+            vmem((2, 2, 4, ZROWS, QS[1]), BF),
+            vmem((2, NX, OWN, QS[0]), BF),
+            vmem((2, NX, OWN, QS[1]), BF),
             vmem((4, OWN, FD), F32),
-            vmem((R, FD), BF),
+            vmem((2, R, FS[0]), BF),
             pltpu.SemaphoreType.DMA((N_SEM,)),
             pltpu.SemaphoreType.DMA((N_SEM,)),
             pltpu.SemaphoreType.DMA((16,)),
         ],
         compiler_params=pltpu.CompilerParams(
-            collective_id=0, has_side_effects=True, vmem_limit_bytes=36 * 1024 * 1024
+            collective_id=0, has_side_effects=True, vmem_limit_bytes=40 * 1024 * 1024
         ),
     )(*(pltpu.with_memory_space_constraint(v, pltpu.HBM) for v in operands))
     small = jax.ShapeDtypeStruct((OWN, FD), F32)
@@ -592,15 +630,16 @@
             small,
             small,
         ),
-        in_specs=[in_vmem] * 8,
+        in_specs=[in_vmem] * 11,
         out_specs=(hbm,) * 6,
         scratch_shapes=[
-            vmem((FD, BR), BF),
+            vmem((BR, FS[1]), BF),
+            vmem((FS[1], BR), BF),
             vmem((2, 2, OWN, FD), F32),
-            pltpu.SemaphoreType.DMA((5 + FD // TILE,)),
+            pltpu.SemaphoreType.DMA((4 + 4 * NX,)),
         ],
         compiler_params=pltpu.CompilerParams(vmem_limit_bytes=16 * 1024 * 1024),
-    )(d_up, steps_down, grads, basis_down, *moments)
+    )(*kept, basis_up, basis_down, *moments)
 
 
 def solution(mesh):

time: 123 us -> 117 us (0.951)
  Pallas kernels: 122 us -> 116 us
    pallas_call x1, Pallas kernels: 119 us -> 114 us  [local(): pl.pallas_call(kernel, out_shape=(vmem((2, R, FS[1]), BF), vmem((BR, FS[0...]
where the time goes in v3:
time: 117 us
  Pallas kernels  116 us (99%)
    pallas_call x1, Pallas kernels, local(): pl.pallas_call(kernel, out_shape=(vmem((2, R, FS[1]), BF), vmem((BR, FS[0...  114 us

profile of v3, /device:TPU:1, one launch (start us, length us, event | category | flops | bytes accessed | tf_op | source)
XLA Modules:
  0.0 116.6 jit_solution(5708600665199394801)
XLA Ops:
  0.6 0.0 copy-start.5
  0.6 0.0 copy-start.4
  0.7 0.0 copy-start.3
  0.7 0.0 copy-start.2
  0.7 0.0 copy-start.1
  0.7 0.0 copy-start
  0.7 113.5 %shard_map.145 = (bf16[2,512,1536]{2,1,0:T(8,128)(2,1)S(1)}, bf16[256,2048]{1,0:T(8,128)(2,1)S(1)}, bf16[2048,256]{1,0:T(8,128)(2,1)S(1)}, bf16[2,16,2048]{2,1,0:T(8,128)(2,1)S(1)}, bf16[2,16,1536]{2,1,0:T(8,128)(2,1)S(1)}) custom-call(bf16[128,8192]{1,0:T(8,128)(2,1)} %tokens.1, bf16[128,8192]{1,0:T(8,128)(2,1)} %out_grad.1, bf16[128,3584]{1,0:T(8,128)(2,1)} %up_grad.1, ...), custom_call_target="tpu_custom_call" | custom-call | tf_op jit(solution)/shard_map/pallas_call | solution.py:586
  114.2 0.0 copy-done.5
  114.3 0.0 copy-done.4
  114.3 0.0 copy-done.3
  114.3 0.0 copy-done.2
  114.3 0.0 copy-done.1
  114.3 0.0 copy-done
  114.3 2.3 %shard_map.146 = (bf16[256,3584]{1,0:T(8,128)(2,1)}, bf16[3584,256]{1,0:T(8,128)(2,1)}, f32[16,3584]{1,0:T(8,128)}, f32[16,3584]{1,0:T(8,128)}, f32[16,3584]{1,0:T(8,128)}, /*index=5*/f32[16,3584]{1,0:T(8,128)}) custom-call(bf16[2,512,1536]{2,1,0:T(8,128)(2,1)S(1)} %get-tuple-element.11.steps1, bf16[256,2048]{1,0:T(8,128)(2,1)S(1)} %get-tuple-element.12.d_up0, ...), custom_call_target="tpu_custom_call" | custom-call | tf_op jit(solution)/shard_map/pallas_call | solution.py:623
Async XLA Ops:
  0.6 113.6 %copy-start.5 = (f32[16,3584]{1,0:T(8,128)S(1)}, f32[16,3584]{1,0:T(8,128)}, u32[]{:S(2)}) copy-start(f32[16,3584]{1,0:T(8,128)} %v_down.3) | copy-start | bytes 688132
  0.6 113.6 %copy-start.4 = (f32[16,3584]{1,0:T(8,128)S(1)}, f32[16,3584]{1,0:T(8,128)}, u32[]{:S(2)}) copy-start(f32[16,3584]{1,0:T(8,128)} %m_down.3) | copy-start | bytes 688132
  0.7 113.6 %copy-start.3 = (f32[16,3584]{1,0:T(8,128)S(1)}, f32[16,3584]{1,0:T(8,128)}, u32[]{:S(2)}) copy-start(f32[16,3584]{1,0:T(8,128)} %v_up.3) | copy-start | bytes 688132
  0.7 113.6 %copy-start.2 = (f32[16,3584]{1,0:T(8,128)S(1)}, f32[16,3584]{1,0:T(8,128)}, u32[]{:S(2)}) copy-start(f32[16,3584]{1,0:T(8,128)} %m_up.3) | copy-start | bytes 688132
  0.7 113.6 %copy-start.1 = (bf16[256,512]{1,0:T(8,128)(2,1)S(1)}, bf16[256,512]{1,0:T(8,128)(2,1)}, u32[]{:S(2)}) copy-start(bf16[256,512]{1,0:T(8,128)(2,1)} %basis_down.3) | copy-start | bytes 786436
  0.7 113.6 %copy-start = (bf16[256,512]{1,0:T(8,128)(2,1)S(1)}, bf16[256,512]{1,0:T(8,128)(2,1)}, u32[]{:S(2)}) copy-start(bf16[256,512]{1,0:T(8,128)(2,1)} %basis_up.3) | copy-start | bytes 786436

commit v4 on v3

--- a/solution.py
+++ b/solution.py
@@ -27,6 +27,7 @@
 ZROWS = NX * OWN
 QS, QO = (512, 384), (0, 512)
 FS = tuple(NX * w for w in QS)
+DEPTH = 2
 W1 = (1280, 896)
 TILE = 512
 N_SEM = 320
@@ -86,6 +87,15 @@
 
     used = [0]
     pending = []
+    slow = []
+    done = [0]
+    marks = []
+
+    def drain():
+        marks.append(len(pending))
+        for cp in pending[done[0] : marks[-DEPTH]] if len(marks) >= DEPTH else ():
+            cp.wait_send()
+            done[0] += 1
 
     def take(n):
         used[0] += n
@@ -101,11 +111,11 @@
             device_id_type=MESH,
         )
 
-    def send(src, dst, dev, k=None, rk=None):
+    def send(src, dst, dev, k=None, rk=None, sent=pending):
         k = take(1) if k is None else k
         cp = remote(src, dst, dev, k, k if rk is None else rk)
         cp.start()
-        pending.append(cp)
+        sent.append(cp)
         return cp
 
     def landed(ref, rk):
@@ -142,7 +152,7 @@
 
     y_cols = pl.ds(pl.multiple_of(y * RY, RY), RY)
 
-    b_reg0 = b_all.at[x, z]
+    b_reg0 = b_all.at[z, 0]
     own_b = load_by_core(basis_up.at[:, y_cols], basis_down.at[:, y_cols], b_reg0)
     own_t = load_by_core(tokens, out_grad, t_buf)
     ins = (up_grad, hidden)
@@ -164,13 +174,63 @@
 
     dirs = (1, -1)
 
-    def b_reg(xo, zo, half=None):
-        ref = b_all.at[wrap(x + xo, NX), wrap(z + zo, NZ)]
-        if half is None:
-            return ref
-        return ref.at[pl.ds(half * (BR // 2), BR // 2), :]
-
-    def gather_xz(reg, direct):
+    OWN_X, SIDES, FAR = slice(0, 1), slice(1, 3), slice(3, 4)
+    offset = (0, -1, 1, 2)
+
+    def gather_basis():
+        hx, hz = {}, {}
+
+        def z_send(who, d, k, half=None):
+            rows = slice(None) if half is None else pl.ds(half * (BR // 2), BR // 2)
+            blk = b_all.at[wrap(z - d * (k - 1), NZ), who, rows, :]
+            hz[who.start, d, k] = send(blk, blk, at(zo=d))
+
+        def z_step(who, k):
+            for d in dirs:
+                hz[who.start, d, k].wait_recv()
+                if k < 4:
+                    z_send(who, d, k + 1, None if k < 3 else (0 if d > 0 else 1))
+            slots = range(who.start, who.stop)
+            return [(i, zo) for i in slots for zo in ((-k, k) if k < 4 else (4,))]
+
+        def r0():
+            for k, (i, xo) in enumerate(((1, 1), (2, -1), (3, 2))):
+                hx[i] = send(b_all.at[z, 0], b_all.at[z, i], at(xo=xo))
+            for d in dirs:
+                z_send(OWN_X, d, 1)
+            return [(0, 0)]
+
+        def r1():
+            hx[1].wait_recv()
+            hx[2].wait_recv()
+            for d in dirs:
+                z_send(SIDES, d, 1)
+            return [(1, 0), (2, 0)]
+
+        def r2():
+            got = z_step(OWN_X, 1)
+            hx[3].wait_recv()
+            for d in dirs:
+                z_send(FAR, d, 1)
+            return got + [(3, 0)]
+
+        def later(pairs):
+            def run():
+                return [b for who, k in pairs for b in z_step(who, k)]
+
+            return run
+
+        return [
+            r0,
+            r1,
+            r2,
+            later([(SIDES, 1), (OWN_X, 2), (FAR, 1)]),
+            later([(SIDES, 2), (OWN_X, 3), (FAR, 2)]),
+            later([(SIDES, 3), (OWN_X, 4), (FAR, 3)]),
+            later([(SIDES, 4), (FAR, 4)]),
+        ]
+
+    def gather_xz(reg):
         hx, hz = {}, {}
 
         def z_first(xb):
@@ -191,28 +251,22 @@
             blk = reg(0, 0)
             for d in dirs:
                 hx[d, 1] = send(blk, blk, at(xo=d))
-            if direct:
-                hx[2] = send(blk, blk, at(xo=2))
             z_first(0)
             return [(0, 0)]
 
         def r1():
             for d in dirs:
                 hx[d, 1].wait_recv()
-                if not direct:
-                    blk = reg(-d, 0, 0 if d > 0 else 1)
-                    hx[d, 2] = send(blk, blk, at(xo=d))
+                blk = reg(-d, 0, 0 if d > 0 else 1)
+                hx[d, 2] = send(blk, blk, at(xo=d))
             z_first(-1)
             z_first(1)
             return [(-1, 0), (1, 0)]
 
         def r2():
             done = z_step(0, 1)
-            if direct:
-                hx[2].wait_recv()
-            else:
-                for d in dirs:
-                    hx[d, 2].wait_recv()
+            for d in dirs:
+                hx[d, 2].wait_recv()
             z_first(2)
             return done + [(2, 0)]
 
@@ -225,16 +279,6 @@
 
             return run
 
-        if direct:
-            return [
-                r0,
-                r1,
-                r2,
-                later([(-1, 1), (1, 1), (0, 2), (2, 1)]),
-                later([(-1, 2), (1, 2), (0, 3), (2, 2)]),
-                later([(-1, 3), (1, 3), (0, 4), (2, 3)]),
-                later([(-1, 4), (1, 4), (2, 4)]),
-            ]
         return [
             r0,
             r1,
@@ -247,10 +291,10 @@
         ]
 
     def project(blocks):
-        for xo, zo in blocks:
-            xx, zz = wrap(x + xo, NX), wrap(z + zo, NZ)
+        for i, zo in blocks:
+            xx, zz = wrap(x + offset[i], NX), wrap(z + zo, NZ)
             cols = pl.ds(pl.multiple_of((xx * NZ + zz) * BR, BR), BR)
-            acc[...] += jnp.dot(t_buf[:, cols], b_all[xx, zz], preferred_element_type=F32)
+            acc[...] += jnp.dot(t_buf[:, cols], b_all[zz, i], preferred_element_type=F32)
 
     x1 = x + 1 - 2 * lax.rem(x, 2)
     x3 = NX - 1 - x
@@ -262,18 +306,18 @@
     def core_dev(xx, m):
         return (xx * NZ + z, y * 2 + m)
 
-    rounds = gather_xz(b_reg, True)
+    rounds = gather_basis()
     blocks = rounds[0]()
     got_b, got_a, got_c = take(2), take(2), take(2)
     for m in (0, 1):
         p1, p2 = near[m]
-        send(ins[m].at[:, quarter(x2)], relay.at[c], core_dev(p1, m), rk=got_b + c)
+        send(ins[m].at[:, quarter(x2)], relay.at[c], core_dev(p1, m), rk=got_b + c, sent=slow)
     for m in (0, 1):
         p1, p2 = near[m]
-        send(ins[m].at[:, quarter(p1)], u_buf.at[c, tok_rows(x), :], core_dev(p1, m), rk=got_a + c)
+        send(ins[m].at[:, quarter(p1)], u_buf.at[c, tok_rows(x), :], core_dev(p1, m), rk=got_a + c, sent=slow)
     for m in (0, 1):
         p1, p2 = near[m]
-        send(ins[m].at[:, quarter(p2)], u_buf.at[c, tok_rows(x), :], core_dev(p2, m), rk=got_c + c)
+        send(ins[m].at[:, quarter(p2)], u_buf.at[c, tok_rows(x), :], core_dev(p2, m), rk=got_c + c, sent=slow)
     k_own = take(1)
     own_there = [
         remote(ins[m].at[:, quarter(x)], u_buf.at[c, tok_rows(x), :], at(co=1), k_own, k_own)
@@ -288,31 +332,27 @@
     def _():
         own_there[1].start()
 
-    pending.append(own_there[0])
+    slow.append(own_there[0])
     hd = []
     own_t.wait()
     project(blocks)
     for k in range(1, len(rounds)):
         blocks = rounds[k]()
-        if k == 4:
+        if k == 3:
             for h in (0, 1):
                 landed(relay.at[h], got_b + h)
-                hd.append(send(relay.at[h], u_buf.at[h, tok_rows(my_p1), :], x_dev(my_p2)))
+                hd.append(send(relay.at[h], u_buf.at[h, tok_rows(my_p1), :], x_dev(my_p2), sent=slow))
         project(blocks)
+        drain()
 
     mine = pt.at[y_cols, tok_rows(x)]
     mine[...] = acc[...].T.astype(BF)
     hp = {}
-    for xo in (0, 2, 1, -1):
+    for xo in (2, 1, -1, 0):
         for yo in range(NY):
-            if xo == 0 and yo == 0 or xo == 2 and yo > 1:
+            if xo == 0 and yo == 0:
                 continue
             hp[xo, yo] = send(mine, mine, at(xo=xo, yo=yo))
-    hp[1, 0].wait_recv()
-    hp[-1, 0].wait_recv()
-    for yo in (2, 3):
-        blk = pt.at[y_cols, tok_rows(wrap(x + 1, NX))]
-        hp[2, yo] = send(blk, blk, at(xo=-1, yo=yo))
     own_u.wait()
     landed(u_buf.at[1 - c, tok_rows(x), :], k_own)
     for h in (0, 1):
@@ -321,8 +361,7 @@
     for cp in hd:
         cp.wait_recv()
     for key, cp in hp.items():
-        if key not in ((1, 0), (-1, 0)):
-            cp.wait_recv()
+        cp.wait_recv()
 
     def cols_of(st):
         return pl.ds(QO[st], QS[st])
@@ -462,7 +501,7 @@
         return reg
 
     plans = [
-        (gather_xz(s_reg(st, W1[st], FS[st]), False), gather_zx(s_reg(st, 0, W1[st])))
+        (gather_xz(s_reg(st, W1[st], FS[st])), gather_zx(s_reg(st, 0, W1[st])))
         for st in (0, 1)
     ]
 
@@ -482,7 +521,10 @@
         for h in (0, 1):
             gradient(st, h)
             rs_step(st, h, 0)
+    for cp in slow:
+        cp.wait_send()
     for k in range(1, 4):
+        drain()
         for st in (0, 1):
             for h in (0, 1):
                 rs_step(st, h, k)
@@ -497,10 +539,11 @@
     for k in range(1, 7):
         run_round(0, k)
         run_round(1, k)
+        drain()
     run_round(0, 7)
     update()
     run_round(1, 7)
-    for cp in pending:
+    for cp in pending[done[0] :]:
         cp.wait_send()
     assert used[0] <= N_SEM, used[0]
 
@@ -596,7 +639,7 @@
         out_specs=(in_vmem,) * 5,
         scratch_shapes=[
             vmem((TOK, D), BF),
-            vmem((NX, NZ, BR, RY), BF),
+            vmem((NZ, NX, BR, RY), BF),
             vmem((2, BR, R), BF),
             vmem((TOK, RY), F32),
             vmem((2, NX * TOK, Q), BF),

time: 117 us -> 114 us (0.974)
  Pallas kernels: 116 us -> 113 us
    pallas_call x1, Pallas kernels: 114 us -> 111 us  [local(): pl.pallas_call(kernel, out_shape=(vmem((2, R, FS[1]), BF), vmem((BR, FS[0...]
where the time goes in v4:
time: 114 us
  Pallas kernels  113 us (99%)
    pallas_call x1, Pallas kernels, local(): pl.pallas_call(kernel, out_shape=(vmem((2, R, FS[1]), BF), vmem((BR, FS[0...  111 us
    pallas_call x1, Pallas kernels, local(): pl.pallas_call(finish, out_shape=(jax.ShapeDtypeStruct((BR, FD), BF), jax...  2.29 us

profile of v4, /device:TPU:1, one launch (start us, length us, event | category | flops | bytes accessed | tf_op | source)
XLA Modules:
  0.0 114.1 jit_solution(2031079738010055354)
XLA Ops:
  0.6 0.0 copy-start.5
  0.6 0.0 copy-start.4
  0.7 0.0 copy-start.3
  0.7 0.0 copy-start.2
  0.7 0.0 copy-start.1
  0.7 0.0 copy-start
  0.7 111.0 %shard_map.145 = (bf16[2,512,1536]{2,1,0:T(8,128)(2,1)S(1)}, bf16[256,2048]{1,0:T(8,128)(2,1)S(1)}, bf16[2048,256]{1,0:T(8,128)(2,1)S(1)}, bf16[2,16,2048]{2,1,0:T(8,128)(2,1)S(1)}, bf16[2,16,1536]{2,1,0:T(8,128)(2,1)S(1)}) custom-call(bf16[128,8192]{1,0:T(8,128)(2,1)} %tokens.1, bf16[128,8192]{1,0:T(8,128)(2,1)} %out_grad.1, bf16[128,3584]{1,0:T(8,128)(2,1)} %up_grad.1, ...), custom_call_target="tpu_custom_call" | custom-call | tf_op jit(solution)/shard_map/pallas_call | solution.py:629
  111.7 0.0 copy-done.5
  111.8 0.0 copy-done.4
  111.8 0.0 copy-done.3
  111.8 0.0 copy-done.2
  111.8 0.0 copy-done.1
  111.8 0.0 copy-done
  111.8 2.3 %shard_map.146 = (bf16[256,3584]{1,0:T(8,128)(2,1)}, bf16[3584,256]{1,0:T(8,128)(2,1)}, f32[16,3584]{1,0:T(8,128)}, f32[16,3584]{1,0:T(8,128)}, f32[16,3584]{1,0:T(8,128)}, /*index=5*/f32[16,3584]{1,0:T(8,128)}) custom-call(bf16[2,512,1536]{2,1,0:T(8,128)(2,1)S(1)} %get-tuple-element.11.steps1, bf16[256,2048]{1,0:T(8,128)(2,1)S(1)} %get-tuple-element.12.d_up0, ...), custom_call_target="tpu_custom_call" | custom-call | tf_op jit(solution)/shard_map/pallas_call | solution.py:666
Async XLA Ops:
  0.6 111.1 %copy-start.5 = (f32[16,3584]{1,0:T(8,128)S(1)}, f32[16,3584]{1,0:T(8,128)}, u32[]{:S(2)}) copy-start(f32[16,3584]{1,0:T(8,128)} %v_down.3) | copy-start | bytes 688132
  0.6 111.1 %copy-start.4 = (f32[16,3584]{1,0:T(8,128)S(1)}, f32[16,3584]{1,0:T(8,128)}, u32[]{:S(2)}) copy-start(f32[16,3584]{1,0:T(8,128)} %m_down.3) | copy-start | bytes 688132
  0.7 111.1 %copy-start.3 = (f32[16,3584]{1,0:T(8,128)S(1)}, f32[16,3584]{1,0:T(8,128)}, u32[]{:S(2)}) copy-start(f32[16,3584]{1,0:T(8,128)} %v_up.3) | copy-start | bytes 688132
  0.7 111.1 %copy-start.2 = (f32[16,3584]{1,0:T(8,128)S(1)}, f32[16,3584]{1,0:T(8,128)}, u32[]{:S(2)}) copy-start(f32[16,3584]{1,0:T(8,128)} %m_up.3) | copy-start | bytes 688132
  0.7 111.1 %copy-start.1 = (bf16[256,512]{1,0:T(8,128)(2,1)S(1)}, bf16[256,512]{1,0:T(8,128)(2,1)}, u32[]{:S(2)}) copy-start(bf16[256,512]{1,0:T(8,128)(2,1)} %basis_down.3) | copy-start | bytes 786436
  0.7 111.1 %copy-start = (bf16[256,512]{1,0:T(8,128)(2,1)S(1)}, bf16[256,512]{1,0:T(8,128)(2,1)}, u32[]{:S(2)}) copy-start(bf16[256,512]{1,0:T(8,128)(2,1)} %basis_up.3) | copy-start | bytes 786436

commit v5 on v3

--- a/solution.py
+++ b/solution.py
@@ -27,7 +27,8 @@
 ZROWS = NX * OWN
 QS, QO = (512, 384), (0, 512)
 FS = tuple(NX * w for w in QS)
-W1 = (1280, 896)
+DEPTH = 2
+W1 = (1408, 768)
 TILE = 512
 N_SEM = 320
 
@@ -86,6 +87,15 @@
 
     used = [0]
     pending = []
+    slow = []
+    done = [0]
+    marks = []
+
+    def drain():
+        marks.append(len(pending))
+        for cp in pending[done[0] : marks[-DEPTH]] if len(marks) >= DEPTH else ():
+            cp.wait_send()
+            done[0] += 1
 
     def take(n):
         used[0] += n
@@ -101,11 +111,11 @@
             device_id_type=MESH,
         )
 
-    def send(src, dst, dev, k=None, rk=None):
+    def send(src, dst, dev, k=None, rk=None, sent=pending):
         k = take(1) if k is None else k
         cp = remote(src, dst, dev, k, k if rk is None else rk)
         cp.start()
-        pending.append(cp)
+        sent.append(cp)
         return cp
 
     def landed(ref, rk):
@@ -230,9 +240,9 @@
                 r0,
                 r1,
                 r2,
-                later([(-1, 1), (1, 1), (0, 2), (2, 1)]),
-                later([(-1, 2), (1, 2), (0, 3), (2, 2)]),
-                later([(-1, 3), (1, 3), (0, 4), (2, 3)]),
+                later([(-1, 1), (1, 1), (2, 1), (0, 2)]),
+                later([(-1, 2), (1, 2), (2, 2), (0, 3)]),
+                later([(-1, 3), (1, 3), (2, 3), (0, 4)]),
                 later([(-1, 4), (1, 4), (2, 4)]),
             ]
         return [
@@ -267,13 +277,13 @@
     got_b, got_a, got_c = take(2), take(2), take(2)
     for m in (0, 1):
         p1, p2 = near[m]
-        send(ins[m].at[:, quarter(x2)], relay.at[c], core_dev(p1, m), rk=got_b + c)
+        send(ins[m].at[:, quarter(x2)], relay.at[c], core_dev(p1, m), rk=got_b + c, sent=slow)
     for m in (0, 1):
         p1, p2 = near[m]
-        send(ins[m].at[:, quarter(p1)], u_buf.at[c, tok_rows(x), :], core_dev(p1, m), rk=got_a + c)
+        send(ins[m].at[:, quarter(p1)], u_buf.at[c, tok_rows(x), :], core_dev(p1, m), rk=got_a + c, sent=slow)
     for m in (0, 1):
         p1, p2 = near[m]
-        send(ins[m].at[:, quarter(p2)], u_buf.at[c, tok_rows(x), :], core_dev(p2, m), rk=got_c + c)
+        send(ins[m].at[:, quarter(p2)], u_buf.at[c, tok_rows(x), :], core_dev(p2, m), rk=got_c + c, sent=slow)
     k_own = take(1)
     own_there = [
         remote(ins[m].at[:, quarter(x)], u_buf.at[c, tok_rows(x), :], at(co=1), k_own, k_own)
@@ -288,31 +298,27 @@
     def _():
         own_there[1].start()
 
-    pending.append(own_there[0])
+    slow.append(own_there[0])
     hd = []
     own_t.wait()
     project(blocks)
     for k in range(1, len(rounds)):
         blocks = rounds[k]()
-        if k == 4:
+        if k == 3:
             for h in (0, 1):
                 landed(relay.at[h], got_b + h)
-                hd.append(send(relay.at[h], u_buf.at[h, tok_rows(my_p1), :], x_dev(my_p2)))
+                hd.append(send(relay.at[h], u_buf.at[h, tok_rows(my_p1), :], x_dev(my_p2), sent=slow))
         project(blocks)
+        drain()
 
     mine = pt.at[y_cols, tok_rows(x)]
     mine[...] = acc[...].T.astype(BF)
     hp = {}
-    for xo in (0, 2, 1, -1):
+    for xo in (2, 1, -1, 0):
         for yo in range(NY):
-            if xo == 0 and yo == 0 or xo == 2 and yo > 1:
+            if xo == 0 and yo == 0:
                 continue
             hp[xo, yo] = send(mine, mine, at(xo=xo, yo=yo))
-    hp[1, 0].wait_recv()
-    hp[-1, 0].wait_recv()
-    for yo in (2, 3):
-        blk = pt.at[y_cols, tok_rows(wrap(x + 1, NX))]
-        hp[2, yo] = send(blk, blk, at(xo=-1, yo=yo))
     own_u.wait()
     landed(u_buf.at[1 - c, tok_rows(x), :], k_own)
     for h in (0, 1):
@@ -321,8 +327,7 @@
     for cp in hd:
         cp.wait_recv()
     for key, cp in hp.items():
-        if key not in ((1, 0), (-1, 0)):
-            cp.wait_recv()
+        cp.wait_recv()
 
     def cols_of(st):
         return pl.ds(QO[st], QS[st])
@@ -482,7 +487,10 @@
         for h in (0, 1):
             gradient(st, h)
             rs_step(st, h, 0)
+    for cp in slow:
+        cp.wait_send()
     for k in range(1, 4):
+        drain()
         for st in (0, 1):
             for h in (0, 1):
                 rs_step(st, h, k)
@@ -497,10 +505,11 @@
     for k in range(1, 7):
         run_round(0, k)
         run_round(1, k)
+        drain()
     run_round(0, 7)
     update()
     run_round(1, 7)
-    for cp in pending:
+    for cp in pending[done[0] :]:
         cp.wait_send()
     assert used[0] <= N_SEM, used[0]
 

time: 117 us -> 114 us (0.974)
  Pallas kernels: 116 us -> 113 us
    pallas_call x1, Pallas kernels: 114 us -> 111 us  [local(): pl.pallas_call(kernel, out_shape=(vmem((2, R, FS[1]), BF), vmem((BR, FS[0...]
where the time goes in v5:
time: 114 us
  Pallas kernels  113 us (99%)
    pallas_call x1, Pallas kernels, local(): pl.pallas_call(kernel, out_shape=(vmem((2, R, FS[1]), BF), vmem((BR, FS[0...  111 us
    pallas_call x1, Pallas kernels, local(): pl.pallas_call(finish, out_shape=(jax.ShapeDtypeStruct((BR, FD), BF), jax...  2.29 us

profile of v5, /device:TPU:1, one launch (start us, length us, event | category | flops | bytes accessed | tf_op | source)
XLA Modules:
  0.0 113.8 jit_solution(17230224448179804126)
XLA Ops:
  0.6 0.0 copy-start.5
  0.6 0.0 copy-start.4
  0.7 0.0 copy-start.3
  0.7 0.0 copy-start.2
  0.7 0.0 copy-start.1
  0.7 0.0 copy-start
  0.7 110.8 %shard_map.145 = (bf16[2,512,1536]{2,1,0:T(8,128)(2,1)S(1)}, bf16[256,2048]{1,0:T(8,128)(2,1)S(1)}, bf16[2048,256]{1,0:T(8,128)(2,1)S(1)}, bf16[2,16,2048]{2,1,0:T(8,128)(2,1)S(1)}, bf16[2,16,1536]{2,1,0:T(8,128)(2,1)S(1)}) custom-call(bf16[128,8192]{1,0:T(8,128)(2,1)} %tokens.1, bf16[128,8192]{1,0:T(8,128)(2,1)} %out_grad.1, bf16[128,3584]{1,0:T(8,128)(2,1)} %up_grad.1, ...), custom_call_target="tpu_custom_call" | custom-call | tf_op jit(solution)/shard_map/pallas_call | solution.py:595
  111.5 0.0 copy-done.5
  111.5 0.0 copy-done.4
  111.5 0.0 copy-done.3
  111.5 0.0 copy-done.2
  111.5 0.0 copy-done.1
  111.5 0.0 copy-done
  111.5 2.3 %shard_map.146 = (bf16[256,3584]{1,0:T(8,128)(2,1)}, bf16[3584,256]{1,0:T(8,128)(2,1)}, f32[16,3584]{1,0:T(8,128)}, f32[16,3584]{1,0:T(8,128)}, f32[16,3584]{1,0:T(8,128)}, /*index=5*/f32[16,3584]{1,0:T(8,128)}) custom-call(bf16[2,512,1536]{2,1,0:T(8,128)(2,1)S(1)} %get-tuple-element.11.steps1, bf16[256,2048]{1,0:T(8,128)(2,1)S(1)} %get-tuple-element.12.d_up0, ...), custom_call_target="tpu_custom_call" | custom-call | tf_op jit(solution)/shard_map/pallas_call | solution.py:632
Async XLA Ops:
  0.6 110.8 %copy-start.5 = (f32[16,3584]{1,0:T(8,128)S(1)}, f32[16,3584]{1,0:T(8,128)}, u32[]{:S(2)}) copy-start(f32[16,3584]{1,0:T(8,128)} %v_down.3) | copy-start | bytes 688132
  0.6 110.8 %copy-start.4 = (f32[16,3584]{1,0:T(8,128)S(1)}, f32[16,3584]{1,0:T(8,128)}, u32[]{:S(2)}) copy-start(f32[16,3584]{1,0:T(8,128)} %m_down.3) | copy-start | bytes 688132
  0.7 110.8 %copy-start.3 = (f32[16,3584]{1,0:T(8,128)S(1)}, f32[16,3584]{1,0:T(8,128)}, u32[]{:S(2)}) copy-start(f32[16,3584]{1,0:T(8,128)} %v_up.3) | copy-start | bytes 688132
  0.7 110.8 %copy-start.2 = (f32[16,3584]{1,0:T(8,128)S(1)}, f32[16,3584]{1,0:T(8,128)}, u32[]{:S(2)}) copy-start(f32[16,3584]{1,0:T(8,128)} %m_up.3) | copy-start | bytes 688132
  0.7 110.8 %copy-start.1 = (bf16[256,512]{1,0:T(8,128)(2,1)S(1)}, bf16[256,512]{1,0:T(8,128)(2,1)}, u32[]{:S(2)}) copy-start(bf16[256,512]{1,0:T(8,128)(2,1)} %basis_down.3) | copy-start | bytes 786436
  0.7 110.8 %copy-start = (bf16[256,512]{1,0:T(8,128)(2,1)S(1)}, bf16[256,512]{1,0:T(8,128)(2,1)}, u32[]{:S(2)}) copy-start(bf16[256,512]{1,0:T(8,128)(2,1)} %basis_up.3) | copy-start | bytes 786436

commit v6 on v5

--- a/solution.py
+++ b/solution.py
@@ -47,6 +47,7 @@
     steps1,
     d_up,
     d_down,
+    new,
     gr0,
     gr1,
     t_buf,
@@ -388,6 +389,8 @@
                 grad = gr[st][m, :, here].astype(F32)
                 moment = momentum_decay * mom[2 * m, :, cols] + (1.0 - momentum_decay) * grad
                 second = square_decay * mom[2 * m + 1, :, cols] + (1.0 - square_decay) * grad * grad
+                new[2 * m, :, cols] = moment
+                new[2 * m + 1, :, cols] = second
                 step = (
                     update_scale
                     * (moment * (1.0 / first_fix))
@@ -518,14 +521,9 @@
     steps1,
     d_up0,
     d_down0,
-    gr0,
-    gr1,
+    new,
     basis_up,
     basis_down,
-    m_up,
-    v_up,
-    m_down,
-    v_down,
     delta_up,
     delta_down,
     next_m_up,
@@ -534,7 +532,6 @@
     next_v_down,
     d_up,
     d_down,
-    new,
     sem,
 ):
     cps = []
@@ -551,18 +548,8 @@
         here, there = places(0, q)
         store(d_up0.at[:, here], delta_up.at[:, there])
         store(d_down0.at[here, :], delta_down.at[there, :])
-    old = ((m_up, v_up), (m_down, v_down))
-    outs = ((next_m_up, next_v_up), (next_m_down, next_v_down))
-    for k in (0, 1):
-        for st, gr in enumerate((gr0, gr1)):
-            for q in range(NX):
-                here, there = places(st, q)
-                grad = gr[k, :, here].astype(F32)
-                moment, second = old[k][0][:, there], old[k][1][:, there]
-                new[k, 0, :, there] = momentum_decay * moment + (1.0 - momentum_decay) * grad
-                new[k, 1, :, there] = square_decay * second + (1.0 - square_decay) * grad * grad
-        for j in (0, 1):
-            store(new.at[k, j], outs[k][j])
+    for k, out in enumerate((next_m_up, next_v_up, next_m_down, next_v_down)):
+        store(new.at[k], out)
     for q in range(NX):
         here, there = places(1, q)
         val = jnp.dot(basis_down[...], steps1[1, :, here], preferred_element_type=F32)
@@ -598,12 +585,13 @@
             vmem((2, R, FS[1]), BF),
             vmem((BR, FS[0]), BF),
             vmem((FS[0], BR), BF),
+            vmem((4, OWN, FD), F32),
+        ),
+        in_specs=[hbm] * 10,
+        out_specs=(in_vmem,) * 4,
+        scratch_shapes=[
             vmem((2, OWN, FS[0]), BF),
             vmem((2, OWN, FS[1]), BF),
-        ),
-        in_specs=[hbm] * 10,
-        out_specs=(in_vmem,) * 5,
-        scratch_shapes=[
             vmem((TOK, D), BF),
             vmem((NX, NZ, BR, RY), BF),
             vmem((2, BR, R), BF),
@@ -639,16 +627,15 @@
             small,
             small,
         ),
-        in_specs=[in_vmem] * 11,
+        in_specs=[in_vmem] * 6,
         out_specs=(hbm,) * 6,
         scratch_shapes=[
             vmem((BR, FS[1]), BF),
             vmem((FS[1], BR), BF),
-            vmem((2, 2, OWN, FD), F32),
             pltpu.SemaphoreType.DMA((4 + 4 * NX,)),
         ],
         compiler_params=pltpu.CompilerParams(vmem_limit_bytes=16 * 1024 * 1024),
-    )(*kept, basis_up, basis_down, *moments)
+    )(*kept, basis_up, basis_down)
 
 
 def solution(mesh):

time: 114 us -> 114 us (level)
  no operation moved by 1% of the time
where the time goes in v6:
time: 114 us
  Pallas kernels  113 us (99%)
    pallas_call x1, Pallas kernels, local(): pl.pallas_call(kernel, out_shape=(vmem((2, R, FS[1]), BF), vmem((BR, FS[0...  111 us
    pallas_call x1, Pallas kernels, local(): pl.pallas_call(finish, out_shape=(jax.ShapeDtypeStruct((BR, FD), BF), jax...  2.31 us

profile of v6, /device:TPU:1, one launch (start us, length us, event | category | flops | bytes accessed | tf_op | source)
XLA Modules:
  0.0 113.8 jit_solution(12366781593879083350)
XLA Ops:
  0.6 0.0 copy-start.1
  0.6 0.0 copy-start
  0.7 110.8 %shard_map.145 = (bf16[2,512,1536]{2,1,0:T(8,128)(2,1)S(1)}, bf16[256,2048]{1,0:T(8,128)(2,1)S(1)}, bf16[2048,256]{1,0:T(8,128)(2,1)S(1)}, f32[4,16,3584]{2,1,0:T(8,128)S(1)}) custom-call(bf16[128,8192]{1,0:T(8,128)(2,1)} %tokens.1, bf16[128,8192]{1,0:T(8,128)(2,1)} %out_grad.1, bf16[128,3584]{1,0:T(8,128)(2,1)} %up_grad.1, bf16[128,3584]{1,0:T(8,128)(2,1)} %hidden.1, ...), custom_call_target="tpu_custom_call" | custom-call | tf_op jit(solution)/shard_map/pallas_call | solution.py:582
  111.4 0.0 copy-done.1
  111.4 0.0 copy-done
  111.4 2.3 %shard_map.146 = (bf16[256,3584]{1,0:T(8,128)(2,1)}, bf16[3584,256]{1,0:T(8,128)(2,1)}, f32[16,3584]{1,0:T(8,128)}, f32[16,3584]{1,0:T(8,128)}, f32[16,3584]{1,0:T(8,128)}, /*index=5*/f32[16,3584]{1,0:T(8,128)}) custom-call(bf16[2,512,1536]{2,1,0:T(8,128)(2,1)S(1)} %get-tuple-element.10.steps1, bf16[256,2048]{1,0:T(8,128)(2,1)S(1)} %get-tuple-element.11.d_up0, ...), custom_call_target="tpu_custom_call" | custom-call | tf_op jit(solution)/shard_map/pallas_call | solution.py:620
Async XLA Ops:
  0.6 110.8 %copy-start.1 = (bf16[256,512]{1,0:T(8,128)(2,1)S(1)}, bf16[256,512]{1,0:T(8,128)(2,1)}, u32[]{:S(2)}) copy-start(bf16[256,512]{1,0:T(8,128)(2,1)} %basis_down.3) | copy-start | bytes 786436
  0.6 110.8 %copy-start = (bf16[256,512]{1,0:T(8,128)(2,1)S(1)}, bf16[256,512]{1,0:T(8,128)(2,1)}, u32[]{:S(2)}) copy-start(bf16[256,512]{1,0:T(8,128)(2,1)} %basis_up.3) | copy-start | bytes 786436
